TPU v7x, 32 devices: a whole 2x2x4 slice. The times are simulated.
32 devices in a mesh: dp: 8 (over z, x), seq: 4 (over y, core).
Axes of the slice: x: 2, y: 2, z: 4, core: 2. Of those that a mesh axis runs over, the one named last changes fastest.
Arguments:
- inputs: bfloat16 [8, 1024, 768], P('dp', 'seq'), may hold values from -6 to 6
- w_query: bfloat16 [768, 768], replicated, may hold values from -0.21875 to 0.21875
- query_bias: bfloat16 [768], replicated, may hold values from -4 to 4
- w_key: bfloat16 [768, 768], replicated, may hold values from -0.21875 to 0.21875
- w_value: bfloat16 [768, 768], replicated, may hold values from -0.21875 to 0.21875
- value_bias: bfloat16 [768], replicated, may hold values from -0.75 to 0.75
- w_proj: bfloat16 [768, 768], replicated, may hold values from -3 to 3
- proj_bias: bfloat16 [768], replicated, may hold values from -4 to 4
- ln1_gain: bfloat16 [768], replicated, may hold values from 0.5 to 1.5
- ln1_bias: bfloat16 [768], replicated, may hold values from -4 to 4
- w_up: bfloat16 [768, 3072], replicated, may hold values from -0.21875 to 0.21875
- up_bias: bfloat16 [3072], replicated, may hold values from -4 to 4
- w_down: bfloat16 [3072, 768], replicated, may hold values from -0.109375 to 0.109375
- down_bias: bfloat16 [768], replicated, may hold values from -4 to 4
- ln2_gain: bfloat16 [768], replicated, may hold values from 0.5 to 1.5
- ln2_bias: bfloat16 [768], replicated, may hold values from -4 to 4
- long_group: int32 [8], P('dp'), may hold values from 0 to 1, as said below
- random_blocks: int32 [8, 16, 3], P('dp', 'seq'), may hold values from 1 to 14, as said below
- out_grad: bfloat16 [8, 1024, 768], P('dp', 'seq'), may hold values from -6 to 6
Outputs:
- layer_out: bfloat16 [8, 1024, 768], P('dp', 'seq')
- input_grad: float32 [8, 1024, 768], P('dp', 'seq')
- grad_w_query: float32 [768, 768], P('seq')
- grad_w_key: float32 [768, 768], P('seq')
- grad_w_value: float32 [768, 768], P('seq')
- grad_w_proj: float32 [768, 768], P('seq')
- grad_w_up: float32 [768, 3072], P('seq')
- grad_w_down: float32 [3072, 768], P('seq')
- grad_query_bias: float32 [768], replicated
- grad_value_bias: float32 [768], replicated
- grad_proj_bias: float32 [768], replicated
- grad_ln1_gain: float32 [768], replicated
- grad_ln1_bias: float32 [768], replicated
- grad_up_bias: float32 [3072], replicated
- grad_down_bias: float32 [768], replicated
- grad_ln2_gain: float32 [768], replicated
- grad_ln2_bias: float32 [768], replicated
Inputs may be any that keep to these rules, and one draw needn't show every extreme that they name: `long_group`: 1 marks a group holding one sequence of 1024 tokens, 0 a group holding 2 sequences of 512 tokens. `random_blocks`: for a block at relative position p of its sequence of n blocks, the 3 entries are distinct positions of the same sequence, none of them 0, n - 1, p - 1, p or p + 1; the entries of global blocks are not used.
All inputs are finite; a program needn't handle non-finite values.
Results may differ from a plain program's by a relative error of at most 0.018.
Values may be sent and summed in bfloat16 or wider, within the bound.
No kernel may reach another device: no remote copies, remote signals or barrier semaphores. Data moves between devices by JAX's collectives and lax.ppermute only.
A program may use at most 192 MiB of HBM per device.

v0:
```python
import jax
import jax.numpy as jnp
from jax import lax
from jax.sharding import PartitionSpec as P

D = 768
HEADS = 12
HEAD = 64
FF = 3072
BLOCK = 64
RAND = 3
SLOTS = 2
SLOT_TOK = 128
T_DEV = 256


LN_EPS = 1e-05
MASKED = -1e30


def layer_norm(residual, ln_gain, ln_shift):
    center = residual - jnp.mean(residual, axis=-1, keepdims=True)
    variance = jnp.mean(center * center, axis=-1, keepdims=True)
    return center * lax.rsqrt(variance + LN_EPS) * ln_gain + ln_shift


def gelu_tanh(pre_act):
    return jax.nn.gelu(pre_act, approximate=True)


def seq_coords(blocks, is_long, per_slot, per_dev):
    device = blocks // per_dev
    within = blocks % per_dev
    slot_id = jnp.where(is_long, 0, within // per_slot)
    position = jnp.where(is_long, blocks, device * per_slot + within % per_slot)
    return (slot_id, position)


def to_group(slot_id, position, is_long, per_slot, per_dev):
    placed = position // per_slot * per_dev + slot_id * per_slot + position % per_slot
    return jnp.where(is_long, position, placed)


def key_plan(blocks, chosen, is_long, per_slot, per_dev, total_blocks):
    slot_id, position = seq_coords(blocks, is_long, per_slot, per_dev)
    last_pos = jnp.where(is_long, total_blocks, total_blocks // SLOTS).astype(jnp.int32) - 1
    first_pos = jnp.zeros_like(position)
    before = jnp.clip(position - 1, 0, last_pos)
    after = jnp.clip(position + 1, 0, last_pos)
    fixed_pos = jnp.stack([first_pos, first_pos + last_pos, before, position, after], axis=-1)
    relative = jnp.concatenate([fixed_pos, chosen], axis=-1)
    targets = to_group(slot_id[:, None], relative, is_long, per_slot, per_dev)
    all_true = position >= 0
    fixed_ok = jnp.stack(
        [all_true, all_true, position != 1, all_true, position + 1 != last_pos], axis=-1
    )
    allowed = jnp.concatenate(
        [fixed_ok, jnp.broadcast_to(all_true[:, None], chosen.shape)], axis=-1
    )
    is_global = (position == 0) | (position == last_pos)
    return (targets, allowed, is_global)


def global_plan(device, is_long, per_slot, per_dev, seq_devices):
    slot_ids = jnp.arange(SLOTS, dtype=jnp.int32)
    at_end = device == seq_devices - 1
    at_start = device == 0
    cand_rows = slot_ids * per_slot + jnp.where(at_end, per_slot - 1, 0)
    cand_blocks = device * per_dev + cand_rows
    long_flags = at_start & (slot_ids == 0) | at_end & (slot_ids == SLOTS - 1)
    short_flags = (at_start | at_end) & (slot_ids >= 0)
    return (cand_rows, cand_blocks, jnp.where(is_long, long_flags, short_flags))


def row_stats(scores):
    row_peak = jnp.max(scores, axis=-1, keepdims=True)
    row_total = jnp.sum(jnp.exp(scores - row_peak), axis=-1, keepdims=True)
    return (row_peak, row_total)


def sparse_scores(query_b, key_blocks, key_mask):
    scores = jnp.einsum("bqhd,bkhd->bhqk", query_b, key_blocks, preferred_element_type=jnp.float32)
    return jnp.where(key_mask, scores, MASKED)


def global_scores(query_g, key_heads, same_seq):
    scores = jnp.einsum("cqhd,khd->chqk", query_g, key_heads, preferred_element_type=jnp.float32)
    return jnp.where(same_seq, scores, MASKED)


def on_device(
    inputs,
    w_query,
    query_bias,
    w_key,
    w_value,
    value_bias,
    w_proj,
    proj_bias,
    ln1_gain,
    ln1_bias,
    w_up,
    up_bias,
    w_down,
    down_bias,
    ln2_gain,
    ln2_bias,
    long_group,
    random_blocks,
    out_grad,
):
    n_seq = lax.axis_size("seq")
    n_dp = lax.axis_size("dp")
    device = lax.axis_index("seq")
    tok_rows = inputs.reshape(T_DEV, D)
    is_long = long_group[0] == 1
    per_slot = SLOT_TOK // BLOCK
    per_dev = T_DEV // BLOCK
    total_blocks = per_dev * n_seq
    group_tok = T_DEV * n_seq
    key_width = (5 + RAND) * BLOCK
    query_rows = (
        (jnp.dot(tok_rows, w_query, preferred_element_type=jnp.float32) + query_bias) * 0.125
    ).astype(jnp.bfloat16)
    key_own = jnp.dot(tok_rows, w_key, preferred_element_type=jnp.float32).astype(jnp.bfloat16)
    value_own = (
        jnp.dot(tok_rows, w_value, preferred_element_type=jnp.float32) + value_bias
    ).astype(jnp.bfloat16)
    key_group, value_group = (
        lax.all_gather(key_own, "seq", axis=0, tiled=True),
        lax.all_gather(value_own, "seq", axis=0, tiled=True),
    )
    blocks = device * per_dev + jnp.arange(per_dev, dtype=jnp.int32)
    targets, allowed, is_global = key_plan(
        blocks, random_blocks[0], is_long, per_slot, per_dev, total_blocks
    )
    query_b = query_rows.reshape(per_dev, BLOCK, HEADS, HEAD)
    key_blocks = key_group.reshape(total_blocks, BLOCK, D)[targets].reshape(
        per_dev, key_width, HEADS, HEAD
    )
    value_blocks = value_group.reshape(total_blocks, BLOCK, D)[targets].reshape(
        per_dev, key_width, HEADS, HEAD
    )
    key_mask = jnp.repeat(allowed, BLOCK, axis=1)[:, None, None, :]
    scores = sparse_scores(query_b, key_blocks, key_mask)
    row_peak, row_total = row_stats(scores)
    attn_probs = (jnp.exp(scores - row_peak) / row_total).astype(jnp.bfloat16)
    sparse_out = jnp.einsum(
        "bhqk,bkhd->bqhd", attn_probs, value_blocks, preferred_element_type=jnp.float32
    )
    cand_rows, cand_blocks, cand_flags = global_plan(device, is_long, per_slot, per_dev, n_seq)
    all_blocks = jnp.arange(total_blocks, dtype=jnp.int32)
    slot_all = seq_coords(all_blocks, is_long, per_slot, per_dev)[0]
    same_seq = jnp.repeat(slot_all[None, :] == slot_all[cand_blocks][:, None], BLOCK, axis=1)[
        :, None, None, :
    ]
    key_heads = key_group.reshape(group_tok, HEADS, HEAD)
    value_heads = value_group.reshape(group_tok, HEADS, HEAD)
    query_g = query_b[cand_rows]
    has_global = jnp.any(cand_flags)

    def global_forward():
        glob_scores = global_scores(query_g, key_heads, same_seq)
        glob_peak, glob_total = row_stats(glob_scores)
        glob_probs = (jnp.exp(glob_scores - glob_peak) / glob_total).astype(jnp.bfloat16)
        glob_out = jnp.einsum(
            "chqk,khd->cqhd", glob_probs, value_heads, preferred_element_type=jnp.float32
        )
        return (glob_out, glob_peak, glob_total)

    def global_skip():
        stat_shape = (SLOTS, HEADS, BLOCK, 1)
        return (
            jnp.zeros((SLOTS, BLOCK, HEADS, HEAD), jnp.float32),
            jnp.zeros(stat_shape, jnp.float32),
            jnp.ones(stat_shape, jnp.float32),
        )

    glob_out, glob_peak, glob_total = lax.cond(has_global, global_forward, global_skip)
    picked = jnp.where(cand_flags[:, None, None, None], glob_out, sparse_out[cand_rows])
    attended = sparse_out.at[cand_rows].set(picked).reshape(T_DEV, D)
    mixed = attended.astype(jnp.bfloat16)
    attn_out = jnp.dot(mixed, w_proj, preferred_element_type=jnp.float32) + proj_bias
    resid_one = tok_rows.astype(jnp.float32) + attn_out
    normed, ln1_pull = jax.vjp(
        layer_norm, resid_one, ln1_gain.astype(jnp.float32), ln1_bias.astype(jnp.float32)
    )
    normed_low = normed.astype(jnp.bfloat16)
    hidden_pre = jnp.dot(normed_low, w_up, preferred_element_type=jnp.float32) + up_bias
    activated, gelu_pull = jax.vjp(gelu_tanh, hidden_pre)
    hidden = activated.astype(jnp.bfloat16)
    branch = jnp.dot(hidden, w_down, preferred_element_type=jnp.float32) + down_bias
    final_out, ln2_pull = jax.vjp(
        layer_norm, normed + branch, ln2_gain.astype(jnp.float32), ln2_bias.astype(jnp.float32)
    )
    layer_out = final_out.astype(jnp.bfloat16).reshape(1, T_DEV, D)
    cotangent = out_grad.reshape(T_DEV, D).astype(jnp.float32)
    d_resid2, d_gain2, d_bias2 = ln2_pull(cotangent)
    d_branch = d_resid2.astype(jnp.bfloat16)
    grad_down_w = jnp.einsum("tf,td->fd", hidden, d_branch, preferred_element_type=jnp.float32)
    grad_down_b = jnp.sum(d_branch.astype(jnp.float32), axis=0)
    d_hidden = jnp.einsum("td,fd->tf", d_branch, w_down, preferred_element_type=jnp.float32).astype(
        jnp.bfloat16
    )
    (d_pre_raw,) = gelu_pull(d_hidden.astype(jnp.float32))
    d_pre = d_pre_raw.astype(jnp.bfloat16)
    grad_up_w = jnp.einsum("td,tf->df", normed_low, d_pre, preferred_element_type=jnp.float32)
    grad_up_b = jnp.sum(d_pre.astype(jnp.float32), axis=0)
    d_normed = d_resid2 + jnp.einsum("tf,df->td", d_pre, w_up, preferred_element_type=jnp.float32)
    d_resid1, d_gain1, d_bias1 = ln1_pull(d_normed)
    d_attn = d_resid1.astype(jnp.bfloat16)
    grad_proj_w = jnp.einsum("td,te->de", mixed, d_attn, preferred_element_type=jnp.float32)
    grad_proj_b = jnp.sum(d_attn.astype(jnp.float32), axis=0)
    d_mixed = jnp.einsum("te,de->td", d_attn, w_proj, preferred_element_type=jnp.float32).astype(
        jnp.bfloat16
    )
    d_mixed = d_mixed.reshape(per_dev, BLOCK, HEADS, HEAD)
    zero_grad = jnp.zeros_like(d_mixed)
    dout_sparse = jnp.where(is_global[:, None, None, None], zero_grad, d_mixed)
    scores_again = sparse_scores(query_b, key_blocks, key_mask)
    probs_full = jnp.exp(scores_again - row_peak) / row_total
    d_probs = jnp.einsum(
        "bqhd,bkhd->bhqk", dout_sparse, value_blocks, preferred_element_type=jnp.float32
    )
    row_delta = jnp.sum(probs_full * d_probs, axis=-1, keepdims=True)
    d_scores = (probs_full * (d_probs - row_delta)).astype(jnp.bfloat16)
    d_query = jnp.einsum(
        "bhqk,bkhd->bqhd", d_scores, key_blocks, preferred_element_type=jnp.float32
    )
    dout_glob = jnp.where(cand_flags[:, None, None, None], d_mixed[cand_rows], zero_grad[cand_rows])

    def global_back():
        glob_scores = global_scores(query_g, key_heads, same_seq)
        glob_probs = jnp.exp(glob_scores - glob_peak) / glob_total
        glob_dprobs = jnp.einsum(
            "cqhd,khd->chqk", dout_glob, value_heads, preferred_element_type=jnp.float32
        )
        glob_delta = jnp.sum(glob_probs * glob_dprobs, axis=-1, keepdims=True)
        glob_dscores = (glob_probs * (glob_dprobs - glob_delta)).astype(jnp.bfloat16)
        glob_dquery = jnp.einsum(
            "chqk,khd->cqhd", glob_dscores, key_heads, preferred_element_type=jnp.float32
        )
        glob_dkey = jnp.einsum(
            "chqk,cqhd->khd", glob_dscores, query_g, preferred_element_type=jnp.float32
        )
        glob_dvalue = jnp.einsum(
            "chqk,cqhd->khd",
            glob_probs.astype(jnp.bfloat16),
            dout_glob,
            preferred_element_type=jnp.float32,
        )
        return (
            glob_dquery,
            glob_dkey.reshape(group_tok, D),
            glob_dvalue.reshape(group_tok, D),
            glob_delta,
        )

    def global_none():
        return (
            jnp.zeros((SLOTS, BLOCK, HEADS, HEAD), jnp.float32),
            jnp.zeros((group_tok, D), jnp.float32),
            jnp.zeros((group_tok, D), jnp.float32),
            jnp.zeros((SLOTS, HEADS, BLOCK, 1), jnp.float32),
        )

    glob_dquery, glob_dkey, glob_dvalue, glob_delta = lax.cond(has_global, global_back, global_none)
    d_query = d_query.at[cand_rows].add(glob_dquery)
    d_key_blocks = jnp.einsum(
        "bhqk,bqhd->bkhd", d_scores, query_b, preferred_element_type=jnp.float32
    )
    d_value_blocks = jnp.einsum(
        "bhqk,bqhd->bkhd",
        probs_full.astype(jnp.bfloat16),
        dout_sparse,
        preferred_element_type=jnp.float32,
    )
    block_shape = (per_dev, 5 + RAND, BLOCK, D)
    key_buffer = (
        jnp.zeros((total_blocks, BLOCK, D), jnp.float32)
        .at[targets]
        .add(d_key_blocks.reshape(block_shape))
    )
    value_buffer = (
        jnp.zeros((total_blocks, BLOCK, D), jnp.float32)
        .at[targets]
        .add(d_value_blocks.reshape(block_shape))
    )
    key_total = key_buffer.reshape(group_tok, D) + glob_dkey
    value_total = value_buffer.reshape(group_tok, D) + glob_dvalue
    key_back, value_back = (
        lax.psum_scatter(
            key_total.astype(jnp.bfloat16), "seq", scatter_dimension=0, tiled=True
        ).astype(jnp.float32),
        lax.psum_scatter(
            value_total.astype(jnp.bfloat16), "seq", scatter_dimension=0, tiled=True
        ).astype(jnp.float32),
    )
    d_key = key_back.astype(jnp.bfloat16)
    d_value = value_back.astype(jnp.bfloat16)
    d_query_low = d_query.reshape(T_DEV, D).astype(jnp.bfloat16)
    grad_query_w = (
        jnp.einsum("td,te->de", tok_rows, d_query_low, preferred_element_type=jnp.float32) * 0.125
    )
    grad_query_b = jnp.sum(d_query_low.astype(jnp.float32), axis=0) * 0.125
    grad_key_w = jnp.einsum("td,te->de", tok_rows, d_key, preferred_element_type=jnp.float32)
    grad_value_w = jnp.einsum("td,te->de", tok_rows, d_value, preferred_element_type=jnp.float32)
    grad_value_b = jnp.sum(d_value.astype(jnp.float32), axis=0)
    input_grad = d_resid1 + 0.125 * jnp.einsum(
        "te,de->td", d_query_low, w_query, preferred_element_type=jnp.float32
    )
    input_grad = input_grad + jnp.einsum(
        "te,de->td", d_key, w_key, preferred_element_type=jnp.float32
    )
    input_grad = input_grad + jnp.einsum(
        "te,de->td", d_value, w_value, preferred_element_type=jnp.float32
    )
    weight_terms = (grad_query_w, grad_key_w, grad_value_w, grad_proj_w, grad_up_w, grad_down_w)
    spread = [
        jnp.transpose(weight_term.reshape(n_seq, n_dp, -1), (1, 0, 2)).reshape(-1)
        for weight_term in weight_terms
    ]
    pieces = (
        lax.psum_scatter(spread[0], ("dp", "seq"), scatter_dimension=0, tiled=True),
        lax.psum_scatter(spread[1], ("dp", "seq"), scatter_dimension=0, tiled=True),
        lax.psum_scatter(spread[2], ("dp", "seq"), scatter_dimension=0, tiled=True),
        lax.psum_scatter(spread[3], ("dp", "seq"), scatter_dimension=0, tiled=True),
        lax.psum_scatter(spread[4], ("dp", "seq"), scatter_dimension=0, tiled=True),
        lax.psum_scatter(spread[5], ("dp", "seq"), scatter_dimension=0, tiled=True),
    )
    shards = (
        lax.all_gather(pieces[0].astype(jnp.bfloat16), "dp", axis=0, tiled=True).astype(
            jnp.float32
        ),
        lax.all_gather(pieces[1].astype(jnp.bfloat16), "dp", axis=0, tiled=True).astype(
            jnp.float32
        ),
        lax.all_gather(pieces[2].astype(jnp.bfloat16), "dp", axis=0, tiled=True).astype(
            jnp.float32
        ),
        lax.all_gather(pieces[3].astype(jnp.bfloat16), "dp", axis=0, tiled=True).astype(
            jnp.float32
        ),
        lax.all_gather(pieces[4].astype(jnp.bfloat16), "dp", axis=0, tiled=True).astype(
            jnp.float32
        ),
        lax.all_gather(pieces[5].astype(jnp.bfloat16), "dp", axis=0, tiled=True).astype(
            jnp.float32
        ),
    )
    results = [
        shard_piece.reshape(weight_term.shape[0] // n_seq, weight_term.shape[1])
        for shard_piece, weight_term in zip(shards, weight_terms)
    ]
    small_terms = jnp.concatenate(
        [
            grad_query_b,
            grad_value_b,
            grad_proj_b,
            d_gain1,
            d_bias1,
            grad_up_b,
            grad_down_b,
            d_gain2,
            d_bias2,
        ]
    )
    summed = lax.psum(small_terms, ("dp", "seq"))
    up_end = 5 * D + FF
    return (
        layer_out,
        input_grad.reshape(1, T_DEV, D),
        results[0],
        results[1],
        results[2],
        results[3],
        results[4],
        results[5],
        summed[0:D],
        summed[D : 2 * D],
        summed[2 * D : 3 * D],
        summed[3 * D : 4 * D],
        summed[4 * D : 5 * D],
        summed[5 * D : up_end],
        summed[up_end : up_end + D],
        summed[up_end + D : up_end + 2 * D],
        summed[up_end + 2 * D : up_end + 3 * D],
    )


def solution(mesh):
    placed = (
        P("dp", "seq", None),
        P(),
        P(),
        P(),
        P(),
        P(),
        P(),
        P(),
        P(),
        P(),
        P(),
        P(),
        P(),
        P(),
        P(),
        P(),
        P("dp"),
        P("dp", "seq", None),
        P("dp", "seq", None),
    )
    return jax.shard_map(
        on_device,
        mesh=mesh,
        in_specs=placed,
        out_specs=(
            P("dp", "seq", None),
            P("dp", "seq", None),
            P("seq", None),
            P("seq", None),
            P("seq", None),
            P("seq", None),
            P("seq", None),
            P("seq", None),
            P(),
            P(),
            P(),
            P(),
            P(),
            P(),
            P(),
            P(),
            P(),
        ),
        check_vma=False,
    )
```

profile of v0, /device:TPU:0, one launch (start us, length us, event | category | flops | bytes accessed | tf_op | source)
XLA Modules:
  0.0 1066.1 jit_solution(12429213102612437884)
XLA Ops:
  8.2 2.6 fusion.50
  10.9 2.6 convolution_convert_fusion.2
  24.4 8.9 all-gather.5.cloned.1.call-done
  33.3 3.8 gather_fusion.2
  37.1 10.6 reshape.1060
  47.7 9.4 copy.169
  57.1 3.8 gather_fusion.3
  60.9 10.6 reshape.1061
  71.5 9.4 copy.168
  81.0 6.3 fusion.89
  87.2 4.8 fusion.42
  94.8 3.0 gather_fusion.6
  97.8 2.6 copy.170
  102.0 10.0 conditional.2
  102.3 2.4 fusion.92
  105.8 2.8 fusion
  112.0 2.6 broadcast_select_fusion.2
  120.2 3.9 convolution_add_fusion
  129.4 14.8 %convert_reduce_fusion = (f32[3072]{0:T(1024)}, bf16[256,3072]{1,0:T(8,128)(2,1)S(1)}) fusion(f32[256,3072]{1,0:T(8,128)S(1)} %convolution_add_fusion, bf16[256,768]{1,0:T(8,128)(2,1)S(1)} %get-tuple-element.165, bf16[3072,768]{1,0:T(8,128)(2,1)S(1)} %bitcast.262), kind=kOutput, calls=%fused_computation.64 | convolution fusion | flops 1226830848 | bytes 9842688 | tf_op jit(solution)/shard_map/td,fd->tf/dot_general | solution.py:202
  150.8 6.2 multiply_reduce_fusion
  159.8 3.7 convolution_bitcast_fusion.1
  163.5 13.6 %copy.210 = f32[4,512,12,64]{3,2,1,0:T(8,128)} copy(f32[4,512,12,64]{1,3,2,0:T(8,128)} %convolution_bitcast_fusion.1) | data formatting | bytes 12582912 | tf_op jit(solution)/shard_map/reshape | solution.py:282
  177.0 13.6 %reshape.1058 = f32[32,64,768]{2,1,0:T(8,128)} reshape(f32[4,512,12,64]{3,2,1,0:T(8,128)} %copy.210) | data formatting | bytes 12582912 | tf_op jit(solution)/shard_map/reshape | solution.py:282
  190.7 41.5 %conditional.3 = (f32[2,64,12,64]{3,1,2,0:T(8,128)S(1)}, f32[1024,768]{1,0:T(8,128)}, f32[1024,768]{1,0:T(8,128)}) conditional(s32[]{:T(128)} %convert_element_type.165, () %tuple.28, (pred[2,1,1,1024]{3,0,2,1:T(4,128)(4,1)S(1)}, bf16[1024,12,64]{0,2,1:T(8,128)(2,1)S(1)}, bf16[2,64,12,64]{3,1,2,0:T(8,128)(2,1)S(1)}, f32[2,12,64,1]{2,0,1,3:T(2,128)}, ...), branch_computations={%region_17.18_spmd, %region_18.20_spmd} | conditional | flops 1030323712 | bytes 103671952 | solution.py:267
  190.7 3.6 fusion.93
  196.9 2.6 gather_fusion
  200.6 2.6 gather_fusion.1
  205.7 5.9 fusion.7
  211.6 2.5 fusion.9
  218.4 3.6 copy.217
  222.0 6.2 fusion.10
  228.3 3.7 copy.219
  234.1 16.1 %scatter_fusion.2 = f32[16,64,768]{2,1,0:T(8,128)} fusion(f32[16,64,768]{2,1,0:T(8,128)} %broadcast.2464.clone, s32[32]{0:T(128)S(1)} %reshape.971, f32[32,64,768]{2,1,0:T(8,128)} %reshape.1058), kind=kCustom, calls=%fused_computation.9 | custom fusion | flops 1572864 | bytes 18874496 | tf_op jit(solution)/shard_map/scatter-add | solution.py:282
  250.2 4.3 fusion.36
  254.6 6.5 convolution_bitcast_fusion
  261.1 13.7 %copy.211 = f32[4,512,12,64]{3,2,1,0:T(8,128)} copy(f32[4,512,12,64]{1,3,2,0:T(8,128)} %convolution_bitcast_fusion) | data formatting | bytes 12582912 | tf_op jit(solution)/shard_map/reshape | solution.py:287
  274.8 13.5 %reshape.1059 = f32[32,64,768]{2,1,0:T(8,128)} reshape(f32[4,512,12,64]{3,2,1,0:T(8,128)} %copy.211) | data formatting | bytes 12582912 | tf_op jit(solution)/shard_map/reshape | solution.py:287
  290.3 16.1 %scatter_fusion.3 = f32[16,64,768]{2,1,0:T(8,128)} fusion(f32[16,64,768]{2,1,0:T(8,128)} %broadcast.2464.clone.1, s32[32]{0:T(128)S(1)} %reshape.971, f32[32,64,768]{2,1,0:T(8,128)} %reshape.1059), kind=kCustom, calls=%fused_computation.10 | custom fusion | flops 1572864 | bytes 18874496 | tf_op jit(solution)/shard_map/scatter-add | solution.py:287
  306.4 4.4 fusion.35
  311.9 5.0 convolution_bitcast_fusion.4
  323.1 3.0 copy.195
  326.1 3.1 reshape.917
  329.2 3.2 copy.253
  335.9 2.9 reshape.929
  338.8 3.2 copy.250
  343.9 5.2 fusion.81
  349.1 8.3 reshape.933
  357.4 13.4 %copy.249 = f32[4,8,73728]{2,0,1:T(4,128)} copy(f32[4,8,73728]{2,1,0:T(8,128)} %reshape.933) | data formatting | bytes 18874368 | tf_op jit(solution)/shard_map/reshape | solution.py:320
  370.8 8.8 copy.232
  379.6 5.9 fusion.84
  385.4 8.3 reshape.937
  393.7 13.4 %copy.248 = f32[4,8,73728]{2,0,1:T(4,128)} copy(f32[4,8,73728]{2,1,0:T(8,128)} %reshape.937) | data formatting | bytes 18874368 | tf_op jit(solution)/shard_map/reshape | solution.py:320
  407.1 8.6 copy.233
  417.1 2.9 convolution_bitcast_fusion.3
  423.6 3.2 copy.252
  428.4 2.9 convolution_bitcast_fusion.2
  435.3 3.2 copy.251
  450.7 461.6 %all-reduce.8 = (bf16[589824]{0:T(1024)(128)(2,1)}, bf16[589824]{0:T(1024)(128)(2,1)}, bf16[589824]{0:T(1024)(128)(2,1)}, bf16[589824]{0:T(1024)(128)(2,1)}, bf1...) all-reduce(f32[589824]{0:T(1024)S(1)} %bitcast.236, ...), channel_id=4, replica_groups=mesh['dp'=8,'seq'=4] {'dp','seq'}, use_global_device_ids=true, to_apply=%region_25.26.clone | all-reduce | flops 7087104 | bytes 42541056
  918.3 31.4 %all_gather.26 = bf16[147456]{0:T(1024)(128)(2,1)S(1)} all-gather(bf16[18432]{0:T(1024)(128)(2,1)S(1)} %dynamic-slice.17), channel_id=1, replica_groups=mesh['dp'=8,'seq'=4] {'dp'}, dimensions={0}, use_global_device_ids=true | all-gather | bytes 331776 | tf_op jit(solution)/shard_map/all_gather | solution.py:332
  951.5 31.1 %all_gather.27 = bf16[147456]{0:T(1024)(128)(2,1)S(1)} all-gather(bf16[18432]{0:T(1024)(128)(2,1)S(1)} %dynamic-slice.16), channel_id=1, replica_groups=mesh['dp'=8,'seq'=4] {'dp'}, dimensions={0}, use_global_device_ids=true | all-gather | bytes 331776 | tf_op jit(solution)/shard_map/all_gather | solution.py:335
  984.4 31.2 %all_gather.28 = bf16[147456]{0:T(1024)(128)(2,1)S(1)} all-gather(bf16[18432]{0:T(1024)(128)(2,1)S(1)} %dynamic-slice.15), channel_id=1, replica_groups=mesh['dp'=8,'seq'=4] {'dp'}, dimensions={0}, use_global_device_ids=true | all-gather | bytes 331776 | tf_op jit(solution)/shard_map/all_gather | solution.py:338
  1017.4 30.8 %all_gather.29 = bf16[147456]{0:T(1024)(128)(2,1)S(1)} all-gather(bf16[18432]{0:T(1024)(128)(2,1)S(1)} %dynamic-slice.14), channel_id=1, replica_groups=mesh['dp'=8,'seq'=4] {'dp'}, dimensions={0}, use_global_device_ids=true | all-gather | bytes 331776 | tf_op jit(solution)/shard_map/all_gather | solution.py:341
  1052.4 3.0 reshape.950
  1055.4 3.3 reshape.952
  (319 shorter events, 104.7 us)
Async XLA Ops:
  7.2 110.9 %copy-start = (bf16[768,768]{1,0:T(8,128)(2,1)S(1)}, bf16[768,768]{1,0:T(8,128)(2,1)}, u32[]{:S(2)}) copy-start(bf16[768,768]{1,0:T(8,128)(2,1)} %param.29) | copy-start | bytes 3538948
  7.2 10.4 copy-start.7
  7.2 6.4 copy-start.69
  7.2 7.0 copy-start.62
  7.2 7.6 copy-start.70
  7.2 8.9 copy-start.76
  7.3 10.4 copy-start.71
  7.3 10.4 copy-start.40
  7.3 26.0 %all-gather.5.cloned.1.call-start = ((), (), s32[]{:S(2)}) async-start(), calls=%async_computation.2 | async-start | bytes 1966080 | tf_op jit(solution)/shard_map/all_gather | solution.py:131
  10.8 46.3 %all-gather.7.cloned.1.call-start = ((), (), s32[]{:S(2)}) async-start(), calls=%async_computation.3 | async-start | bytes 1966080 | tf_op jit(solution)/shard_map/all_gather | solution.py:130
  13.5 8.4 copy-start.72
  13.5 8.4 copy-start.73
  13.5 8.4 copy-start.74
  13.5 9.0 copy-start.75
  13.6 403.5 %reduce-scatter.3.cloned.1.call-start = ((), (), s32[]{:S(2)}) async-start(), calls=%async_computation.4 | async-start | bytes 1966080 | tf_op jit(solution)/shard_map/reduce_scatter | solution.py:292
  19.0 62.0 %copy-start.10 = (bf16[4,64,12,64]{3,1,2,0:T(8,128)(2,1)}, bf16[4,64,12,64]{3,1,2,0:T(8,128)(2,1)S(1)}, u32[]{:S(2)}) copy-start(bf16[4,64,12,64]{3,1,2,0:T(8,128)(2,1)S(1)} %copy.167) | copy-start | bytes 1179652
  23.1 14.0 %copy-start.63 = (s32[2]{0:T(128)}, s32[2]{0:T(128)S(1)}, u32[]{:S(2)}) copy-start(s32[2]{0:T(128)S(1)} %fusion.80) | copy-start | bytes 28
  23.8 78.3 %copy-start.12 = (bf16[2,64,12,64]{3,1,2,0:T(8,128)(2,1)}, bf16[2,64,12,64]{3,1,2,0:T(8,128)(2,1)S(1)}, u32[]{:S(2)}) copy-start(bf16[2,64,12,64]{3,1,2,0:T(8,128)(2,1)S(1)} %gather_fusion.5) | copy-start | bytes 589828
  87.2 4.8 copy-start.46
  94.8 5.6 copy-start.4
  112.0 4.0 copy-start.6
  118.1 6.0 copy-start.25
  118.1 6.0 slice-start.2
  119.9 26.6 %copy-start.49 = (f32[256]{0:T(256)}, f32[256]{0:T(256)S(1)}, u32[]{:S(2)}) copy-start(f32[256]{0:T(256)S(1)} %broadcast_multiply_fusion.2) | copy-start | bytes 3076
  120.2 26.4 %copy-start.56 = (f32[256]{0:T(256)}, f32[256]{0:T(256)S(1)}, u32[]{:S(2)}) copy-start(f32[256]{0:T(256)S(1)} %fusion.72) | copy-start | bytes 3076
  120.2 3.9 copy-start.65
  120.2 3.9 slice-start.3
  124.1 5.3 copy-start.18
  127.5 16.7 %slice-start.4 = ((s8[4718592]{0:T(1024)(128)(4,1)}), s8[4194304]{0:T(1024)(128)(4,1)S(1)}, s32[]{:S(2)}) async-start(s8[4718592]{0:T(1024)(128)(4,1)} %bitcast.263), calls=%async_computation.12 | async-start | bytes 8388608
  129.4 14.8 %copy-start.37 = (bf16[256,768]{1,0:T(8,128)(2,1)}, bf16[256,768]{1,0:T(8,128)(2,1)S(1)}, u32[]{:S(2)}) copy-start(bf16[256,768]{1,0:T(8,128)(2,1)S(1)} %get-tuple-element.165) | copy-start | bytes 1179652
  129.4 14.9 %slice-start.5 = ((s8[4718592]{0:T(1024)(128)(4,1)}), s8[524288]{0:T(1024)(128)(4,1)S(1)}, s32[]{:S(2)}) async-start(s8[4718592]{0:T(1024)(128)(4,1)} %bitcast.263), calls=%async_computation.13 | async-start | bytes 1048576
  146.9 3.8 copy-start.60
  150.3 6.6 copy-start.14
  150.3 6.6 slice-start
  150.8 6.2 copy-start.41
  150.8 6.2 slice-start.1
  177.0 13.6 %copy-start.5 = (bf16[1024,768]{0,1:T(8,128)(2,1)S(1)}, bf16[1024,768]{0,1:T(8,128)(2,1)}, u32[]{:S(2)}) copy-start(bf16[1024,768]{0,1:T(8,128)(2,1)} %copy.170) | copy-start | bytes 4718596
  177.0 13.6 %copy-start.13 = (bf16[2,64,12,64]{3,1,2,0:T(8,128)(2,1)S(1)}, bf16[2,64,12,64]{3,1,2,0:T(8,128)(2,1)}, u32[]{:S(2)}) copy-start(bf16[2,64,12,64]{3,1,2,0:T(8,128)(2,1)} %copy-done.12) | copy-start | bytes 589828
  177.0 13.6 %copy-start.15 = (bf16[4,64,12,64]{1,0,3,2:T(4,128)(2,1)S(1)}, bf16[4,64,12,64]{1,0,3,2:T(4,128)(2,1)}, u32[]{:S(2)}) copy-start(bf16[4,64,12,64]{1,0,3,2:T(4,128)(2,1)} %copy-done.14) | copy-start | bytes 1179652
  205.7 5.9 copy-start.3
  250.2 4.4 copy-start.42
  250.2 4.4 copy-start.48
  254.6 173.9 %reduce-scatter.5.cloned.1.call-start = ((), (), s32[]{:S(2)}) async-start(), calls=%async_computation.5 | async-start | bytes 1966080 | tf_op jit(solution)/shard_map/reduce_scatter | solution.py:295
  306.4 4.8 copy-start.28
  310.8 741.7 %all-gather.9.cloned.1.call-start = ((), (), s32[]{:S(2)}) async-start(), calls=%async_computation.6 | async-start | bytes 1327104 | tf_op jit(solution)/shard_map/all_gather | solution.py:344
  321.2 4.9 copy-start.31
  370.8 8.8 copy-start.19
  370.8 8.8 copy-start.38
  438.5 4.4 copy-start.67
  438.5 5.7 copy-start.66
  438.5 7.0 copy-start.58
  438.5 8.3 copy-start.52
  438.5 9.6 copy-start.51
  438.6 10.9 %copy-start.54 = (f32[768]{0:T(1024)S(1)}, f32[768]{0:T(1024)}, u32[]{:S(2)}) copy-start(f32[768]{0:T(1024)} %convert_reduce_fusion.2) | copy-start | bytes 9220
  438.6 12.1 %copy-start.9 = (f32[8,144,4,128]{3,1,2,0:T(8,128)S(1)}, f32[8,144,4,128]{3,1,2,0:T(8,128)}, u32[]{:S(2)}) copy-start(f32[8,144,4,128]{3,1,2,0:T(8,128)} %copy.228) | copy-start | bytes 7077892
  450.7 464.8 %copy-start.17 = (f32[256,768]{1,0:T(8,128)S(1)}, f32[256,768]{1,0:T(8,128)}, u32[]{:S(2)}) copy-start(f32[256,768]{1,0:T(8,128)} %copy-done.16) | copy-start | bytes 2359300
  450.7 464.9 %copy-start.32 = (bf16[256,768]{0,1:T(8,128)(2,1)S(1)}, bf16[256,768]{0,1:T(8,128)(2,1)}, u32[]{:S(2)}) copy-start(bf16[256,768]{0,1:T(8,128)(2,1)} %copy-done.31) | copy-start | bytes 1179652
  450.7 464.9 %copy-start.61 = (f32[256]{0:T(256)S(1)}, f32[256]{0:T(256)}, u32[]{:S(2)}) copy-start(f32[256]{0:T(256)} %copy-done.60) | copy-start | bytes 3076
  913.9 141.5 %all-gather.11.cloned.1.call-start = ((), (), s32[]{:S(2)}) async-start(), calls=%async_computation.7 | async-start | bytes 1327104 | tf_op jit(solution)/shard_map/all_gather | solution.py:347
  917.4 131.9 %copy-start.44 = (f32[9216]{0:T(1024)S(1)}, f32[9216]{0:T(1024)}, u32[]{:S(2)}) copy-start(f32[9216]{0:T(1024)} %get-tuple-element.163) | copy-start | bytes 110596
  917.4 133.1 %copy-start.20 = (bf16[768,768]{1,0:T(8,128)(2,1)S(1)}, bf16[768,768]{1,0:T(8,128)(2,1)}, u32[]{:S(2)}) copy-start(bf16[768,768]{1,0:T(8,128)(2,1)} %param.26) | copy-start | bytes 3538948
  917.4 133.1 %copy-start.33 = (bf16[256,768]{1,0:T(8,128)(2,1)S(1)}, bf16[256,768]{1,0:T(8,128)(2,1)}, u32[]{:S(2)}) copy-start(bf16[256,768]{1,0:T(8,128)(2,1)} %reduce-scatter.3.cloned.1.call-done) | copy-start | bytes 1179652
  982.6 68.4 %copy-start.24 = (bf16[256,768]{1,0:T(8,128)(2,1)S(1)}, bf16[256,768]{1,0:T(8,128)(2,1)}, u32[]{:S(2)}) copy-start(bf16[256,768]{1,0:T(8,128)(2,1)} %reduce-scatter.5.cloned.1.call-done) | copy-start | bytes 1179652
  1051.0 7.8 copy-start.1
  (25 other events, 56.2 us)
Sparse Core Ops, SparseCore 0:
  10.9 22.3 all-gather.4
  35.5 19.6 all-gather.6
  254.7 28.0 reduce-scatter.2
  310.9 27.8 reduce-scatter.4
  914.0 41.5 all-gather.8
  957.6 42.0 all-gather.10
where the time goes:
time: 1080 us; the launch traced here: 1070 us
  blocking collectives  586 us (54%)
  local copies, waits for them, and re-layouts  275 us (25%)
  matrix products  111 us (10%)
  other arithmetic  66.3 us (6%)
  between operations  17.1 us (2%)
    unnamed x1, blocking collectives  462 us
    reshape x9, local copies, waits for them, and re-layouts, on_device(): weight_term.reshape(n_seq, n_dp, -1)  55.9 us
    unnamed x181, local copies, waits for them, and re-layouts  45.7 us
    all_gather x1, blocking collectives, on_device(): lax.all_gather(pieces[0].astype(jnp.bfloat16), 'dp', axis=0, tiled=True)  31.4 us
    all_gather x1, blocking collectives, on_device(): lax.all_gather(pieces[2].astype(jnp.bfloat16), 'dp', axis=0, tiled=True)  31.2 us
    all_gather x1, blocking collectives, on_device(): lax.all_gather(pieces[1].astype(jnp.bfloat16), 'dp', axis=0, tiled=True)  31.1 us
    all_gather x1, blocking collectives, on_device(): lax.all_gather(pieces[3].astype(jnp.bfloat16), 'dp', axis=0, tiled=True)  30.8 us
    reshape x2, local copies, waits for them, and re-layouts, on_device(): d_key_blocks.reshape(block_shape)  27.2 us
  transfers between devices with their start and end apart: 6, of which 1 were waited for; matrix products, arithmetic and copies ran while one was open for 21% of the time, Pallas kernels for 0%

commit v1 on v0

v1 whole, which is shorter than its diff:
```python
import jax
import jax.numpy as jnp
from jax import lax
from jax.experimental import pallas as pl
from jax.experimental.pallas import tpu as pltpu
from jax.sharding import PartitionSpec as P

D = 768
HEADS = 12
HEAD = 64
FF = 3072
BLOCK = 64
RAND = 3
SLOTS = 2
SLOT_TOK = 128
T_DEV = 256
PER_SLOT = SLOT_TOK // BLOCK
PER_DEV = T_DEV // BLOCK

LN_EPS = 1e-05
MASKED = -1e30
F32 = jnp.float32
BF16 = jnp.bfloat16
MIB = 2**20

NN = (((1,), (0,)), ((), ()))
NT = (((1,), (1,)), ((), ()))
TN = (((0,), (0,)), ((), ()))


def dot(left, right, dims=NN):
    return lax.dot_general(left, right, dims, preferred_element_type=F32)


def layer_norm(residual, ln_gain, ln_shift):
    center = residual - jnp.mean(residual, axis=-1, keepdims=True)
    variance = jnp.mean(center * center, axis=-1, keepdims=True)
    return center * lax.rsqrt(variance + LN_EPS) * ln_gain + ln_shift


def gelu_tanh(pre_act):
    return jax.nn.gelu(pre_act, approximate=True)


def seq_coords(blocks, is_long):
    device = blocks // PER_DEV
    within = blocks % PER_DEV
    slot_id = jnp.where(is_long, 0, within // PER_SLOT)
    position = jnp.where(is_long, blocks, device * PER_SLOT + within % PER_SLOT)
    return (slot_id, position)


def block_bias(device, chosen, is_long, n_seq):
    total_blocks = PER_DEV * n_seq
    last_pos = jnp.where(is_long, total_blocks, total_blocks // SLOTS) - 1
    own_slot, own_pos = seq_coords(device * PER_DEV + jnp.arange(PER_DEV), is_long)
    columns = jnp.arange(total_blocks)
    key_ids = (device ^ (columns // PER_DEV)) * PER_DEV + columns % PER_DEV
    key_slot, key_pos = seq_coords(key_ids, is_long)
    same = own_slot[:, None] == key_slot[None, :]
    ends = (key_pos == 0) | (key_pos == last_pos)
    near = jnp.abs(own_pos[:, None] - key_pos[None, :]) <= 1
    drawn = jnp.any(chosen[:, :, None] == key_pos[None, None, :], axis=1)
    is_global = (own_pos == 0) | (own_pos == last_pos)
    keep = same & (is_global[:, None] | ends[None, :] | near | drawn)
    return jnp.where(keep, 0.0, MASKED).astype(F32)


def attn_fwd_kernel(q_ref, k_ref, v_ref, bias_ref, mixed_ref, lse_ref):
    rows, keys = q_ref.shape[0], k_ref.shape[0]
    query, key, value, bias = q_ref[...], k_ref[...], v_ref[...], bias_ref[...]
    first = lax.broadcasted_iota(jnp.int32, (rows, 2 * HEAD), 1) < HEAD
    outs, lses = [], []
    for head in range(2):
        own = jnp.where(first == (head == 0), query, jnp.zeros_like(query))
        scores = dot(own, key, NT).reshape(PER_DEV, BLOCK, keys) + bias[:, None, :]
        scores = scores.reshape(rows, keys)
        peak = jnp.max(scores, axis=1, keepdims=True)
        weight = jnp.exp(scores - peak)
        total = jnp.sum(weight, axis=1, keepdims=True)
        outs.append(dot((weight * (1.0 / total)).astype(BF16), value))
        lses.append(peak + jnp.log(total))
    mixed_ref[...] = jnp.where(first, outs[0], outs[1]).astype(BF16)
    lse_ref[...] = jnp.where(first, lses[0], lses[1])


def attn_bwd_kernel(q_ref, k_ref, v_ref, bias_ref, g_ref, lse_ref, dq_ref, dk_ref, dv_ref):
    rows, keys = q_ref.shape[0], k_ref.shape[0]
    query, key, value, bias, grad = (
        q_ref[...],
        k_ref[...],
        v_ref[...],
        bias_ref[...],
        g_ref[...],
    )
    first = lax.broadcasted_iota(jnp.int32, (rows, 2 * HEAD), 1) < HEAD
    d_query, d_key, d_value = [], None, None
    for head in range(2):
        mine = first == (head == 0)
        own = jnp.where(mine, query, jnp.zeros_like(query))
        own_grad = jnp.where(mine, grad, jnp.zeros_like(grad))
        scores = dot(own, key, NT).reshape(PER_DEV, BLOCK, keys) + bias[:, None, :]
        probs = jnp.exp(scores.reshape(rows, keys) - lse_ref[:, HEAD * head : HEAD * head + 1])
        d_probs = dot(own_grad, value, NT)
        delta = jnp.sum(probs * d_probs, axis=1, keepdims=True)
        d_scores = (probs * (d_probs - delta)).astype(BF16)
        d_query.append(dot(d_scores, key))
        key_term = dot(d_scores, own, TN)
        value_term = dot(probs.astype(BF16), own_grad, TN)
        d_key = key_term if d_key is None else d_key + key_term
        d_value = value_term if d_value is None else d_value + value_term
    dq_ref[...] = jnp.where(first, d_query[0], d_query[1]).astype(BF16)
    dk_ref[...] = d_key.astype(BF16)
    dv_ref[...] = d_value.astype(BF16)


def head_pair(rows):
    return pl.BlockSpec((rows, 2 * HEAD), lambda i: (0, i))


def whole(shape):
    return pl.BlockSpec(shape, lambda *_: (0,) * len(shape))


def attn_fwd(query, key, value, bias):
    rows, keys = query.shape[0], key.shape[0]
    return pl.pallas_call(
        attn_fwd_kernel,
        grid=(HEADS // 2,),
        in_specs=[head_pair(rows), head_pair(keys), head_pair(keys), whole(bias.shape)],
        out_specs=[head_pair(rows), head_pair(rows)],
        out_shape=[
            jax.ShapeDtypeStruct((rows, D), BF16),
            jax.ShapeDtypeStruct((rows, D), F32),
        ],
        compiler_params=pltpu.CompilerParams(vmem_limit_bytes=40 * MIB),
        name="attn_fwd",
    )(query, key, value, bias)


def attn_bwd(query, key, value, bias, grad, lse):
    rows, keys = query.shape[0], key.shape[0]
    return pl.pallas_call(
        attn_bwd_kernel,
        grid=(HEADS // 2,),
        in_specs=[
            head_pair(rows),
            head_pair(keys),
            head_pair(keys),
            whole(bias.shape),
            head_pair(rows),
            head_pair(rows),
        ],
        out_specs=[head_pair(rows), head_pair(keys), head_pair(keys)],
        out_shape=[
            jax.ShapeDtypeStruct((rows, D), BF16),
            jax.ShapeDtypeStruct((keys, D), BF16),
            jax.ShapeDtypeStruct((keys, D), BF16),
        ],
        compiler_params=pltpu.CompilerParams(vmem_limit_bytes=50 * MIB),
        name="attn_bwd",
    )(query, key, value, bias, grad, lse)


def swap(value, axis, mask):
    size = lax.axis_size(axis)
    return lax.ppermute(value, axis, [(i, i ^ mask) for i in range(size)])


def pick(value, index):
    return lax.dynamic_index_in_dim(value, index, 0, keepdims=False)


def reduce_pieces(grad):
    n_seq, n_dp = lax.axis_size("seq"), lax.axis_size("dp")
    seq, dp = lax.axis_index("seq"), lax.axis_index("dp")
    cols = grad.shape[1]
    share = grad.shape[0] // n_seq
    core = seq % 2
    halves = jnp.swapaxes(grad.reshape(n_seq // 2, 2, share, cols), 0, 1)
    total = pick(halves, core) + swap(pick(halves, 1 - core), "seq", 1)
    step = n_seq // 2
    while step > 1:
        step //= 2
        bit = (seq // (2 * step)) % 2
        halves = total.reshape(2, step, share, cols)
        total = pick(halves, bit) + swap(pick(halves, 1 - bit), "seq", 2 * step)
    bit = dp % 2
    halves = total.reshape(2, share // 2, cols)
    total = pick(halves, bit) + swap(pick(halves, 1 - bit), "dp", 1)
    rest = n_dp // 2
    blocks = total.reshape(rest, share // n_dp, cols)
    place = dp // 2
    piece = pick(blocks, place).astype(F32)
    for other in range(1, rest):
        piece = piece + swap(pick(blocks, place ^ other), "dp", 2 * other).astype(F32)
    return piece.astype(BF16)


def gather_pieces(piece):
    rest = lax.axis_size("dp") // 2
    pieces = [None] * (2 * rest)
    for other in range(rest):
        pieces[2 * other] = piece if other == 0 else swap(piece, "dp", 2 * other)
    for other in range(rest):
        pieces[2 * other + 1] = swap(pieces[2 * other], "dp", 1)
    return pieces


def assemble_kernel(place_ref, *refs, widths):
    outs = refs[len(refs) - len(widths) :]
    for piece_ref, index in zip(refs, range(len(refs) - len(widths))):
        rows = piece_ref.shape[0]
        start = pl.multiple_of(place_ref[index] * rows, 8)
        offset = 0
        for out_ref, width in zip(outs, widths):
            out_ref[pl.ds(start, rows), :] = piece_ref[:, offset : offset + width].astype(F32)
            offset += width


def assemble(pieces, widths):
    n_dp = len(pieces)
    dp = lax.axis_index("dp") ^ jnp.arange(n_dp, dtype=jnp.int32)
    places = dp % 2 * (n_dp // 2) + dp // 2
    rows, cols = pieces[0].shape
    if rows % 8:
        stacked = jnp.zeros((n_dp, rows, cols), F32)
        for i, piece in enumerate(pieces):
            stacked = lax.dynamic_update_slice(stacked, piece.astype(F32)[None], (places[i], 0, 0))
        full = stacked.reshape(n_dp * rows, cols)
        cuts = [sum(widths[:i]) for i in range(len(widths))]
        return [full[:, c : c + w] for c, w in zip(cuts, widths)]
    return pl.pallas_call(
        lambda *refs: assemble_kernel(*refs, widths=widths),
        in_specs=[pl.BlockSpec(memory_space=pltpu.SMEM)]
        + [pl.BlockSpec(memory_space=pltpu.VMEM)] * n_dp,
        out_specs=[pl.BlockSpec(memory_space=pltpu.VMEM)] * len(widths),
        out_shape=[jax.ShapeDtypeStruct((n_dp * rows, w), F32) for w in widths],
        compiler_params=pltpu.CompilerParams(vmem_limit_bytes=24 * MIB),
        name="assemble",
    )(places, *pieces)


def on_device(
    inputs,
    w_query,
    query_bias,
    w_key,
    w_value,
    value_bias,
    w_proj,
    proj_bias,
    ln1_gain,
    ln1_bias,
    w_up,
    up_bias,
    w_down,
    down_bias,
    ln2_gain,
    ln2_bias,
    long_group,
    random_blocks,
    out_grad,
):
    n_seq, n_dp = lax.axis_size("seq"), lax.axis_size("dp")
    device = lax.axis_index("seq")
    tok_rows = inputs.reshape(T_DEV, D)
    parts = [tok_rows] + [None] * (n_seq - 1)
    step = n_seq // 2
    while step > 1:
        for j in range(0, n_seq, 2 * step):
            parts[j + step] = swap(parts[j], "seq", step)
        step //= 2
    for j in range(0, n_seq, 2):
        parts[j + 1] = swap(parts[j], "seq", 1)
    tok_group = jnp.concatenate(parts)
    bias = block_bias(device, random_blocks[0], long_group[0] == 1, n_seq)
    bias = jnp.repeat(bias, BLOCK, axis=1)

    query = ((dot(tok_rows, w_query) + query_bias) * 0.125).astype(BF16)
    key = dot(tok_group, w_key).astype(BF16)
    value = (dot(tok_group, w_value) + value_bias).astype(BF16)
    mixed, lse = attn_fwd(query, key, value, bias)
    attn_out = dot(mixed, w_proj) + proj_bias
    resid_one = tok_rows.astype(F32) + attn_out
    normed, ln1_pull = jax.vjp(
        layer_norm, resid_one, ln1_gain.astype(F32), ln1_bias.astype(F32)
    )
    normed_low = normed.astype(BF16)
    hidden_pre = dot(normed_low, w_up) + up_bias
    activated, gelu_pull = jax.vjp(gelu_tanh, hidden_pre)
    hidden = activated.astype(BF16)
    branch = dot(hidden, w_down) + down_bias
    final_out, ln2_pull = jax.vjp(
        layer_norm, normed + branch, ln2_gain.astype(F32), ln2_bias.astype(F32)
    )
    layer_out = final_out.astype(BF16).reshape(1, T_DEV, D)
    d_resid2, d_gain2, d_bias2 = ln2_pull(out_grad.reshape(T_DEV, D).astype(F32))
    d_branch = d_resid2.astype(BF16)
    piece_down = reduce_pieces(dot(hidden, d_branch, TN).astype(BF16))
    grad_down_b = jnp.sum(d_branch.astype(F32), axis=0)
    d_hidden = dot(d_branch, w_down, NT).astype(BF16)
    (d_pre_raw,) = gelu_pull(d_hidden.astype(F32))
    d_pre = d_pre_raw.astype(BF16)
    piece_up = reduce_pieces(dot(normed_low, d_pre, TN).astype(BF16))
    grad_up_b = jnp.sum(d_pre.astype(F32), axis=0)
    d_normed = d_resid2 + dot(d_pre, w_up, NT)
    d_resid1, d_gain1, d_bias1 = ln1_pull(d_normed)
    d_attn = d_resid1.astype(BF16)
    piece_proj = reduce_pieces(dot(mixed, d_attn, TN).astype(BF16))
    grad_proj_b = jnp.sum(d_attn.astype(F32), axis=0)
    d_mixed = dot(d_attn, w_proj, NT).astype(BF16)

    d_query, d_key, d_value = attn_bwd(query, key, value, bias, d_mixed, lse)
    piece_qkv = reduce_pieces(
        jnp.concatenate(
            [
                (dot(tok_rows, d_query, TN) * 0.125).astype(BF16),
                dot(tok_group, d_key, TN).astype(BF16),
                dot(tok_group, d_value, TN).astype(BF16),
            ],
            axis=1,
        )
    )
    grad_query_b = jnp.sum(d_query.astype(F32), axis=0) * 0.125
    grad_value_b = jnp.sum(d_value.astype(F32), axis=0)

    term = (dot(d_key, w_key, NT) + dot(d_value, w_value, NT)).astype(BF16)
    term = term.reshape(n_seq // 2, 2, T_DEV, D)
    total = term[:, 0].astype(F32) + swap(term[:, 1], "seq", 1).astype(F32)
    step = n_seq // 2
    while step > 1:
        step //= 2
        total = total[:step] + swap(total[step:].astype(BF16), "seq", 2 * step).astype(F32)
    input_grad = d_resid1 + 0.125 * dot(d_query, w_query, NT) + total[0]

    small = jnp.concatenate(
        [
            grad_query_b,
            grad_value_b,
            grad_proj_b,
            d_gain1,
            d_bias1,
            grad_up_b,
            grad_down_b,
            d_gain2,
            d_bias2,
        ]
    )
    for axis, size in (("seq", n_seq), ("dp", n_dp)):
        step = 1
        while step < size:
            small = small + swap(small, axis, step)
            step *= 2

    (grad_down,) = assemble(gather_pieces(piece_down), [D])
    (grad_up,) = assemble(gather_pieces(piece_up), [FF])
    (grad_proj,) = assemble(gather_pieces(piece_proj), [D])
    grad_query, grad_key, grad_value = assemble(gather_pieces(piece_qkv), [D, D, D])
    up_end = 5 * D + FF
    return (
        layer_out,
        input_grad.reshape(1, T_DEV, D),
        grad_query,
        grad_key,
        grad_value,
        grad_proj,
        grad_up,
        grad_down,
        small[0:D],
        small[D : 2 * D],
        small[2 * D : 3 * D],
        small[3 * D : 4 * D],
        small[4 * D : 5 * D],
        small[5 * D : up_end],
        small[up_end : up_end + D],
        small[up_end + D : up_end + 2 * D],
        small[up_end + 2 * D : up_end + 3 * D],
    )


def solution(mesh):
    tokens = P("dp", "seq", None)
    return jax.shard_map(
        on_device,
        mesh=mesh,
        in_specs=(tokens,) + (P(),) * 15 + (P("dp"), tokens, tokens),
        out_specs=(tokens, tokens) + (P("seq", None),) * 6 + (P(),) * 9,
        check_vma=False,
    )
```

time: 1080 us -> 304 us (0.28); the launches traced: 1070 us -> 303 us
  blocking collectives: 586 us -> 0 us
  local copies, waits for them, and re-layouts: 275 us -> 16.4 us
  waiting for transfers between devices: 9.06 us -> 128 us
  matrix products: 111 us -> 34.8 us
  starting transfers between devices: 0.65 us -> 72 us
  other arithmetic: 66.3 us -> 17.6 us
  Pallas kernels: 0 us -> 31.4 us
  between operations: 17.1 us -> 2.32 us
    unnamed x1 -> x0, blocking collectives: 462 us -> none
    reshape x26 -> x1, local copies, waits for them, and re-layouts: 162 us -> 0.08 us  [on_device(): bias = jnp.repeat(bias, BLOCK, axis=1)]
    ppermute x0 -> x62, waiting for transfers between devices: none -> 128 us  [swap(): return lax.ppermute(value, axis, [(i, i ^ mask) for i in range(size)])]
    all_gather x4 -> x0, blocking collectives: 124 us -> none  [the longest x1 31.4 us: on_device(): lax.all_gather(pieces[0].astype(jnp.bfloat16), 'dp', axis=0, tiled=True)]
    ppermute x0 -> x62, starting transfers between devices: none -> 72 us  [swap(): return lax.ppermute(value, axis, [(i, i ^ mask) for i in range(size)])]
    dot_general x28 -> x18, matrix products: 99.1 us -> 34.8 us  [dot(): return lax.dot_general(left, right, dims, preferred_element_type=F32)]
    unnamed x181 -> x61, local copies, waits for them, and re-layouts: 45.7 us -> 0.79 us
    scatter-add x3 -> x0, other arithmetic: 33.1 us -> none  [the longest x1 16.1 us: on_device(): key_buffer = jnp.zeros((total_blocks, BLOCK, D), jnp.float32).at[targets]...]
  transfers between devices with their start and end apart: 6 -> 62, of which waited for: 1 -> 21; matrix products, arithmetic and copies ran while one was open for 21% -> 12% of each run, Pallas kernels for 0% -> 2%
where the time goes in v1:
time: 304 us; the launch traced here: 303 us
  waiting for transfers between devices  128 us (42%)
  starting transfers between devices  72 us (24%)
  matrix products  34.8 us (11%)
  Pallas kernels  31.4 us (10%)
  other arithmetic  17.6 us (6%)
  local copies, waits for them, and re-layouts  16.4 us (5%)
    ppermute x62, waiting for transfers between devices, swap(): return lax.ppermute(value, axis, [(i, i ^ mask) for i in range(size)])  128 us
    ppermute x62, starting transfers between devices, swap(): return lax.ppermute(value, axis, [(i, i ^ mask) for i in range(size)])  72 us
    dot_general x18, matrix products, dot(): return lax.dot_general(left, right, dims, preferred_element_type=F32)  34.8 us
    pallas_call x1, Pallas kernels, attn_bwd(): pl.pallas_call(attn_bwd_kernel, grid=(HEADS // 2,), in_specs=[head_pair(r...  14.4 us
    pallas_call x1, Pallas kernels, attn_fwd(): pl.pallas_call(attn_fwd_kernel, grid=(HEADS // 2,), in_specs=[head_pair(r...  9.5 us
    pallas_call x4, Pallas kernels, assemble(): pl.pallas_call(lambda *refs: assemble_kernel(*refs, widths=widths), in_sp...  7.46 us
    squeeze x16, local copies, waits for them, and re-layouts, pick(): return lax.dynamic_index_in_dim(value, index, 0, keepdims=False)  6.77 us
  transfers between devices with their start and end apart: 62, of which 21 were waited for; matrix products, arithmetic and copies ran while one was open for 12% of the time, Pallas kernels for 2%

profile of v1, /device:TPU:0, one launch (start us, length us, event | category | flops | bytes accessed | tf_op | source)
XLA Modules:
  0.0 302.8 jit_solution(11966383587013270696)
XLA Ops:
  0.7 3.0 %collective-permute-start.1 = (bf16[256,768]{1,0:T(8,128)(2,1)}, bf16[256,768]{1,0:T(8,128)(2,1)S(1)}, u32[]{:S(2)}, u32[]{:S(2)}) collective-permute-start(bf16[256,768]{1,0:T(8,128)(2,1)} %bitcast.188), channel_id=1, source_target_pairs={{0,2},{1,3},{2,0},{3,1},{4,6},{5,7},{6,4},{7,5},{8,10},{9,11},{10,... | collective-permute-start | bytes 1179656 | tf_op jit(solution)/shard_map/ppermute | solution.py:167
  5.3 7.7 %collective-permute-done.1 = bf16[256,768]{1,0:T(8,128)(2,1)S(1)} collective-permute-done((bf16[256,768]{1,0:T(8,128)(2,1)}, bf16[256,768]{1,0:T(8,128)(2,1)S(1)}, u32[]{:S(2)}, u32[]{:S(2)}) %collective-permute-start.1) | collective-permute-done | bytes 393248 | tf_op jit(solution)/shard_map/ppermute | solution.py:167
  20.7 1.9 fusion.15.q_ref
  22.6 2.7 convolution_convert_fusion.3.k_ref
  25.4 3.1 %add_convert_fusion.1.v_ref = bf16[1024,768]{1,0:T(8,128)(2,1)S(1)} fusion(bf16[768,768]{1,0:T(8,128)(2,1)S(1)} %copy-done.13, f32[768]{0:T(1024)S(1)} %convert_element_type.200, bf16[256,768]{1,0:T(8,128)(2,1)} %collective-permute-done.2, bf16[256,768]{1,0:T(8,128)(2,1)S(1)} %collective-permute-done.1, bf16[256,768]{1,0:T(8,128)(2,1)} %collective-permute-done, ...), kind=kOutput, calls=%fused_computation.23 | convolution fusion | flops 1215823872 | bytes 4328448 | tf_op jit(solution)/shard_map/dot_general | solution.py:32
  28.5 9.5 %attn_fwd.1 = (bf16[256,768]{1,0:T(8,128)(2,1)S(1)}, f32[256,768]{1,0:T(8,128)S(1)}) custom-call(bf16[256,768]{1,0:T(8,128)(2,1)S(1)} %fusion.15.q_ref, bf16[1024,768]{1,0:T(8,128)(2,1)S(1)} %convolution_convert_fusion.3.k_ref, bf16[1024,768]{1,0:T(8,128)(2,1)S(1)} %add_convert_fusion.1.v_ref, f32[4,1024]{1,0:T(4,128)S(1)} %reshape.422.bias_ref), custom_call_target="tpu_custom_call" | custom-call | tf_op jit(solution)/shard_map/attn_fwd/pallas_call | solution.py:127
  38.9 1.5 convolution_add_fusion
  41.0 2.1 fusion.60
  45.0 3.1 %convert_reduce_fusion = (f32[3072]{0:T(1024)S(1)}, bf16[256,3072]{1,0:T(8,128)(2,1)S(1)}) fusion(f32[256,3072]{1,0:T(8,128)S(1)} %convolution_add_fusion, bf16[256,768]{1,0:T(8,128)(2,1)S(1)} %get-tuple-element.39, bf16[3072,768]{1,0:T(8,128)(2,1)S(1)} %bitcast.196), kind=kOutput, calls=%fused_computation.19 | convolution fusion | flops 1226830848 | bytes 9842688 | tf_op jit(solution)/shard_map/dot_general | solution.py:32
  48.1 1.7 multiply_reduce_fusion
  50.8 14.4 %attn_bwd.1 = (bf16[256,768]{1,0:T(8,128)(2,1)S(1)}, bf16[1024,768]{1,0:T(8,128)(2,1)S(1)}, bf16[1024,768]{1,0:T(8,128)(2,1)}) custom-call(bf16[256,768]{1,0:T(8,128)(2,1)S(1)} %fusion.15.q_ref, bf16[1024,768]{1,0:T(8,128)(2,1)} %copy-done.2, bf16[1024,768]{1,0:T(8,128)(2,1)} %copy-done.3, f32[4,1024]{1,0:T(4,128)S(1)} %reshape.422.bias_ref, ...), custom_call_target="tpu_custom_call" | custom-call | tf_op jit(solution)/shard_map/attn_bwd/pallas_call | solution.py:143
  66.8 3.7 %convolution_convert_fusion.1 = bf16[768,3072]{1,0:T(8,128)(2,1)} fusion(bf16[256,3072]{1,0:T(8,128)(2,1)S(1)} %get-tuple-element.77, f32[256,768]{1,0:T(8,128)S(1)} %get-tuple-element.72, f32[768]{0:T(1024)S(1)} %convert_element_type.204, f32[768]{0:T(1024)S(1)} %convert_element_type.203, f32[256]{0:T(256)S(1)} %fusion.43, f32[256]{0:T(256)S(1)} %broadcast_multiply_fusion.1), kind=kOutput, calls=%fused_computation.1 | convolution fusion | flops 1211301888 | bytes 7086080 | tf_op jit(solution)/shard_map/dot_general | solution.py:32
  70.6 4.5 %convolution_convert_fusion = bf16[3072,768]{1,0:T(8,128)(2,1)} fusion(bf16[256,768]{1,0:T(8,128)(2,1)S(1)} %get-tuple-element.39, f32[256,3072]{1,0:T(8,128)S(1)} %copy-done.18), kind=kOutput, calls=%fused_computation | convolution fusion | flops 1217396736 | bytes 8257536 | tf_op jit(solution)/shard_map/dot_general | solution.py:32
  76.9 1.4 add_convert_fusion
  81.2 2.6 convolution_convert_fusion.5
  83.8 2.6 convolution_convert_fusion.6
  86.4 1.8 collective-permute-start.58
  88.2 2.0 pad_maximum_fusion
  90.2 5.8 %copy.45 = bf16[768,2304]{1,0:T(8,128)(2,1)} copy(bf16[768,2304]{0,1:T(8,128)(2,1)} %pad_maximum_fusion) | data formatting | bytes 7077888 | tf_op jit(solution)/shard_map/concatenate | solution.py:316
  96.0 1.5 collective-permute-start.59
  97.5 1.6 dynamic-slice_bitcast_fusion.2
  100.0 1.6 collective-permute-start.60
  103.3 1.8 dynamic-slice_bitcast_fusion.1
  105.2 2.7 collective-permute-start.61
  107.8 3.4 %collective-permute-done.19 = bf16[1,192,768]{2,1,0:T(8,128)(2,1)S(1)} collective-permute-done((bf16[1,192,768]{2,1,0:T(8,128)(2,1)S(1)}, bf16[1,192,768]{2,1,0:T(8,128)(2,1)S(1)}, u32[]{:S(2)}, u32[]{:S(2)}) %collective-permute-start.19) | collective-permute-done | bytes 294944 | tf_op jit(solution)/shard_map/ppermute | solution.py:167
  111.9 2.0 dynamic-slice_bitcast_fusion
  114.5 2.0 collective-permute-done.20
  116.5 2.5 collective-permute-start.23
  119.3 1.7 collective-permute-start.21
  122.4 1.9 collective-permute-done.22
  125.2 1.6 collective-permute-start.6
  127.7 27.7 %collective-permute-done.6 = bf16[1,192,2304]{2,1,0:T(8,128)(2,1)S(1)} collective-permute-done((bf16[1,192,2304]{2,1,0:T(8,128)(2,1)S(1)}, bf16[1,192,2304]{2,1,0:T(8,128)(2,1)S(1)}, u32[]{:S(2)}, u32[]{:S(2)}) %collective-permute-start.6) | collective-permute-done | bytes 884768 | tf_op jit(solution)/shard_map/ppermute | solution.py:167
  157.0 6.9 %collective-permute-done.7 = bf16[96,2304]{1,0:T(8,128)(2,1)S(1)} collective-permute-done((bf16[96,2304]{1,0:T(8,128)(2,1)S(1)}, bf16[96,2304]{1,0:T(8,128)(2,1)S(1)}, u32[]{:S(2)}, u32[]{:S(2)}) %collective-permute-start.7) | collective-permute-done | bytes 442400 | tf_op jit(solution)/shard_map/ppermute | solution.py:167
  164.0 2.8 collective-permute-start.10
  166.8 13.8 %collective-permute-done.32 = bf16[1,192,3072]{2,1,0:T(8,128)(2,1)S(1)} collective-permute-done((bf16[1,192,3072]{2,1,0:T(8,128)(2,1)S(1)}, bf16[1,192,3072]{2,1,0:T(8,128)(2,1)S(1)}, u32[]{:S(2)}, u32[]{:S(2)}) %collective-permute-start.32) | collective-permute-done | bytes 1179680 | tf_op jit(solution)/shard_map/ppermute | solution.py:167
  181.7 1.6 collective-permute-start.25
  183.4 2.0 collective-permute-done.8
  185.9 17.6 %collective-permute-done.45 = bf16[1,768,768]{2,1,0:T(8,128)(2,1)S(1)} collective-permute-done((bf16[1,768,768]{2,1,0:T(8,128)(2,1)S(1)}, bf16[1,768,768]{2,1,0:T(8,128)(2,1)S(1)}, u32[]{:S(2)}, u32[]{:S(2)}) %collective-permute-start.45) | collective-permute-done | bytes 1179680 | tf_op jit(solution)/shard_map/ppermute | solution.py:167
  203.5 1.7 collective-permute-start.27
  207.0 1.6 collective-permute-start.26
  209.1 2.1 collective-permute-done.29.refs_7_
  211.7 10.6 %collective-permute-done.26.refs_4_ = bf16[24,768]{1,0:T(8,128)(2,1)S(1)} collective-permute-done((bf16[24,768]{1,0:T(8,128)(2,1)S(1)}, bf16[24,768]{1,0:T(8,128)(2,1)S(1)}, u32[]{:S(2)}, u32[]{:S(2)}) %collective-permute-start.26) | collective-permute-done | bytes 36896 | tf_op jit(solution)/shard_map/ppermute | solution.py:167
  223.9 2.8 collective-permute-start.36
  226.7 1.6 collective-permute-start.34
  228.4 1.7 collective-permute-start.14
  230.1 5.2 %collective-permute-start.16 = (bf16[24,2304]{1,0:T(8,128)(2,1)S(1)}, bf16[24,2304]{1,0:T(8,128)(2,1)S(1)}, u32[]{:S(2)}, u32[]{:S(2)}) collective-permute-start(bf16[24,2304]{1,0:T(8,128)(2,1)S(1)} %fusion.35.refs_1_), channel_id=1, source_target_pairs={{0,24},{4,28},{8,16},{12,20},{16,8},{20,12},{24,0},{28,4},{1,25},{... | collective-permute-start | bytes 331784 | tf_op jit(solution)/shard_map/ppermute | solution.py:167
  235.4 9.5 %collective-permute-done.14.refs_5_ = bf16[24,2304]{1,0:T(8,128)(2,1)S(1)} collective-permute-done((bf16[24,2304]{1,0:T(8,128)(2,1)S(1)}, bf16[24,2304]{1,0:T(8,128)(2,1)S(1)}, u32[]{:S(2)}, u32[]{:S(2)}) %collective-permute-start.14) | collective-permute-done | bytes 110624 | tf_op jit(solution)/shard_map/ppermute | solution.py:167
  246.9 2.8 collective-permute-start.49
  249.7 1.6 collective-permute-start.47
  253.5 1.7 collective-permute-done.49
  255.2 3.7 %collective-permute-start.38 = (bf16[24,3072]{1,0:T(8,128)(2,1)S(1)}, bf16[24,3072]{1,0:T(8,128)(2,1)S(1)}, u32[]{:S(2)}, u32[]{:S(2)}) collective-permute-start(bf16[24,3072]{1,0:T(8,128)(2,1)S(1)} %fusion.32.refs_1_), channel_id=1, source_target_pairs={{0,8},{4,12},{8,0},{12,4},{16,24},{20,28},{24,16},{28,20},{1,9},{5... | collective-permute-start | bytes 442376 | tf_op jit(solution)/shard_map/ppermute | solution.py:167
  258.9 1.9 collective-permute-done.48
  260.8 2.0 collective-permute-start.42
  262.9 1.6 collective-permute-start.51
  265.4 2.0 collective-permute-start.55
  267.3 6.6 %collective-permute-done.40.refs_5_ = bf16[24,3072]{1,0:T(8,128)(2,1)S(1)} collective-permute-done((bf16[24,3072]{1,0:T(8,128)(2,1)S(1)}, bf16[24,3072]{1,0:T(8,128)(2,1)S(1)}, u32[]{:S(2)}, u32[]{:S(2)}) %collective-permute-start.40) | collective-permute-done | bytes 147488 | tf_op jit(solution)/shard_map/ppermute | solution.py:167
  273.9 1.9 collective-permute-start.39
  278.0 1.9 collective-permute-start.50
  279.8 6.2 %collective-permute-done.53.refs_5_ = bf16[96,768]{1,0:T(8,128)(2,1)S(1)} collective-permute-done((bf16[96,768]{1,0:T(8,128)(2,1)S(1)}, bf16[96,768]{1,0:T(8,128)(2,1)S(1)}, u32[]{:S(2)}, u32[]{:S(2)}) %collective-permute-start.53) | collective-permute-done | bytes 147488 | tf_op jit(solution)/shard_map/ppermute | solution.py:167
  291.1 1.9 assemble.4
  292.9 2.1 assemble.6
  295.9 3.2 %collective-permute-done.54.refs_6_ = bf16[96,768]{1,0:T(8,128)(2,1)S(1)} collective-permute-done((bf16[96,768]{1,0:T(8,128)(2,1)S(1)}, bf16[96,768]{1,0:T(8,128)(2,1)S(1)}, u32[]{:S(2)}, u32[]{:S(2)}) %collective-permute-start.54) | collective-permute-done | bytes 147488 | tf_op jit(solution)/shard_map/ppermute | solution.py:167
  299.1 1.6 collective-permute-done.56.refs_8_
  300.7 2.1 assemble.7
  (234 shorter events, 47.6 us)
Async XLA Ops:
  0.7 12.4 %collective-permute-start.1 = (bf16[256,768]{1,0:T(8,128)(2,1)}, bf16[256,768]{1,0:T(8,128)(2,1)S(1)}, u32[]{:S(2)}, u32[]{:S(2)}) collective-permute-start(bf16[256,768]{1,0:T(8,128)(2,1)} %bitcast.188), channel_id=1, source_target_pairs={{0,2},{1,3},{2,0},{3,1},{4,6},{5,7},{6,4},{7,5},{8,10},{9,11},{10,... | collective-permute-start | bytes 1179656 | tf_op jit(solution)/shard_map/ppermute | solution.py:167
  3.7 18.9 %collective-permute-start = (bf16[256,768]{1,0:T(8,128)(2,1)}, bf16[256,768]{1,0:T(8,128)(2,1)}, u32[]{:S(2)}, u32[]{:S(2)}) collective-permute-start(bf16[256,768]{1,0:T(8,128)(2,1)} %bitcast.189), channel_id=1, source_target_pairs={{0,1},{1,0},{2,3},{3,2},{4,5},{5,4},{6,7},{7,6},{8,9},{9,8},{10,11... | collective-permute-start | bytes 1179656 | tf_op jit(solution)/shard_map/ppermute | solution.py:167
  13.0 9.6 %collective-permute-start.2 = (bf16[256,768]{1,0:T(8,128)(2,1)S(1)}, bf16[256,768]{1,0:T(8,128)(2,1)}, u32[]{:S(2)}, u32[]{:S(2)}) collective-permute-start(bf16[256,768]{1,0:T(8,128)(2,1)S(1)} %collective-permute-done.1), channel_id=1, source_target_pairs={{0,1},{1,0},{2,3},{3,2},{4,5},{5,4},{6,7},{7,6},{8,9},{9,8},{10,11... | collective-permute-start | bytes 1179656 | tf_op jit(solution)/shard_map/ppermute | solution.py:167
  79.3 40.0 %collective-permute-start.3 = (bf16[2,256,768]{2,1,0:T(8,128)(2,1)}, bf16[2,256,768]{2,1,0:T(8,128)(2,1)}, u32[]{:S(2)}, u32[]{:S(2)}) collective-permute-start(bf16[2,256,768]{2,1,0:T(8,128)(2,1)} %slice_bitcast_fusion), channel_id=1, source_target_pairs={{0,1},{1,0},{2,3},{3,2},{4,5},{5,4},{6,7},{7,6},{8,9},{9,8},{10,11... | collective-permute-start | bytes 2359304 | tf_op jit(solution)/shard_map/ppermute | solution.py:167
  80.5 21.1 %collective-permute-start.18 = (bf16[2,192,768]{2,1,0:T(8,128)(2,1)}, bf16[2,192,768]{2,1,0:T(8,128)(2,1)}, u32[]{:S(2)}, u32[]{:S(2)}) collective-permute-start(bf16[2,192,768]{2,1,0:T(8,128)(2,1)} %dynamic-slice_bitcast_fusion.5), channel_id=1, source_target_pairs={{0,1},{1,0},{2,3},{3,2},{4,5},{5,4},{6,7},{7,6},{8,9},{9,8},{10,11... | collective-permute-start | bytes 1769480 | tf_op jit(solution)/shard_map/ppermute | solution.py:167
  80.8 5.6 %collective-permute-start.57 = (f32[9216]{0:T(1024)S(1)}, f32[9216]{0:T(1024)S(1)}, u32[]{:S(2)}, u32[]{:S(2)}) collective-permute-start(f32[9216]{0:T(1024)S(1)} %constant_dynamic-update-slice_fusion), channel_id=1, source_target_pairs={{0,1},{1,0},{2,3},{3,2},{4,5},{5,4},{6,7},{7,6},{8,9},{9,8},{10,11... | collective-permute-start | bytes 110600 | tf_op jit(solution)/shard_map/ppermute | solution.py:167
  86.4 9.6 %collective-permute-start.58 = (f32[9216]{0:T(1024)S(1)}, f32[9216]{0:T(1024)S(1)}, u32[]{:S(2)}, u32[]{:S(2)}) collective-permute-start(f32[9216]{0:T(1024)S(1)} %add.571), channel_id=1, source_target_pairs={{0,2},{1,3},{2,0},{3,1},{4,6},{5,7},{6,4},{7,5},{8,10},{9,11},{10,... | collective-permute-start | bytes 110600 | tf_op jit(solution)/shard_map/ppermute | solution.py:167
  96.0 4.0 %collective-permute-start.59 = (f32[9216]{0:T(1024)S(1)}, f32[9216]{0:T(1024)S(1)}, u32[]{:S(2)}, u32[]{:S(2)}) collective-permute-start(f32[9216]{0:T(1024)S(1)} %add.572), channel_id=1, source_target_pairs={{0,4},{4,0},{8,12},{12,8},{16,20},{20,16},{24,28},{28,24},{1,5},{5... | collective-permute-start | bytes 110600 | tf_op jit(solution)/shard_map/ppermute | solution.py:167
  99.1 25.8 %collective-permute-start.5 = (bf16[2,192,2304]{2,1,0:T(8,128)(2,1)S(1)}, bf16[2,192,2304]{2,1,0:T(8,128)(2,1)S(1)}, u32[]{:S(2)}, u32[]{:S(2)}) collective-permute-start(bf16[2,192,2304]{2,1,0:T(8,128)(2,1)S(1)} %dynamic-slice_bitcast_fusion.2), channel_id=1, source_target_pairs={{0,1},{1,0},{2,3},{3,2},{4,5},{5,4},{6,7},{7,6},{8,9},{9,8},{10,11... | collective-permute-start | bytes 5308424 | tf_op jit(solution)/shard_map/ppermute | solution.py:167
  100.0 5.2 %collective-permute-start.60 = (f32[9216]{0:T(1024)S(1)}, f32[9216]{0:T(1024)S(1)}, u32[]{:S(2)}, u32[]{:S(2)}) collective-permute-start(f32[9216]{0:T(1024)S(1)} %add.573), channel_id=1, source_target_pairs={{0,8},{4,12},{8,0},{12,4},{16,24},{20,28},{24,16},{28,20},{1,9},{5... | collective-permute-start | bytes 110600 | tf_op jit(solution)/shard_map/ppermute | solution.py:167
  102.7 8.5 %collective-permute-start.19 = (bf16[1,192,768]{2,1,0:T(8,128)(2,1)S(1)}, bf16[1,192,768]{2,1,0:T(8,128)(2,1)S(1)}, u32[]{:S(2)}, u32[]{:S(2)}) collective-permute-start(bf16[1,192,768]{2,1,0:T(8,128)(2,1)S(1)} %constant_dynamic-slice_fusion.2), channel_id=1, source_target_pairs={{0,2},{1,3},{2,0},{3,1},{4,6},{5,7},{6,4},{7,5},{8,10},{9,11},{10,... | collective-permute-start | bytes 884744 | tf_op jit(solution)/shard_map/ppermute | solution.py:167
  105.1 21.7 %collective-permute-start.31 = (bf16[2,192,3072]{2,1,0:T(8,128)(2,1)S(1)}, bf16[2,192,3072]{2,1,0:T(8,128)(2,1)S(1)}, u32[]{:S(2)}, u32[]{:S(2)}) collective-permute-start(bf16[2,192,3072]{2,1,0:T(8,128)(2,1)S(1)} %dynamic-slice_bitcast_fusion.1), channel_id=1, source_target_pairs={{0,1},{1,0},{2,3},{3,2},{4,5},{5,4},{6,7},{7,6},{8,9},{9,8},{10,11... | collective-permute-start | bytes 7077896 | tf_op jit(solution)/shard_map/ppermute | solution.py:167
  105.2 8.7 %collective-permute-start.61 = (f32[9216]{0:T(1024)S(1)}, f32[9216]{0:T(1024)S(1)}, u32[]{:S(2)}, u32[]{:S(2)}) collective-permute-start(f32[9216]{0:T(1024)S(1)} %add.574), channel_id=1, source_target_pairs={{0,16},{4,20},{8,24},{12,28},{16,0},{20,4},{24,8},{28,12},{1,17},{... | collective-permute-start | bytes 110600 | tf_op jit(solution)/shard_map/ppermute | solution.py:167
  111.3 5.2 %collective-permute-start.20 = (bf16[96,768]{1,0:T(8,128)(2,1)S(1)}, bf16[96,768]{1,0:T(8,128)(2,1)S(1)}, u32[]{:S(2)}, u32[]{:S(2)}) collective-permute-start(bf16[96,768]{1,0:T(8,128)(2,1)S(1)} %dynamic-slice_bitcast_fusion.13), channel_id=1, source_target_pairs={{0,4},{4,0},{8,12},{12,8},{16,20},{20,16},{24,28},{28,24},{1,5},{5... | collective-permute-start | bytes 442376 | tf_op jit(solution)/shard_map/ppermute | solution.py:167
  116.5 5.8 %collective-permute-start.23 = (bf16[24,768]{1,0:T(8,128)(2,1)S(1)}, bf16[24,768]{1,0:T(8,128)(2,1)S(1)}, u32[]{:S(2)}, u32[]{:S(2)}) collective-permute-start(bf16[24,768]{1,0:T(8,128)(2,1)S(1)} %get-tuple-element.61), channel_id=1, source_target_pairs={{0,24},{4,28},{8,16},{12,20},{16,8},{20,12},{24,0},{28,4},{1,25},{... | collective-permute-start | bytes 110600 | tf_op jit(solution)/shard_map/ppermute | solution.py:167
  119.1 5.3 %collective-permute-start.22 = (bf16[24,768]{1,0:T(8,128)(2,1)S(1)}, bf16[24,768]{1,0:T(8,128)(2,1)S(1)}, u32[]{:S(2)}, u32[]{:S(2)}) collective-permute-start(bf16[24,768]{1,0:T(8,128)(2,1)S(1)} %get-tuple-element.62), channel_id=1, source_target_pairs={{0,16},{4,20},{8,24},{12,28},{16,0},{20,4},{24,8},{28,12},{1,17},{... | collective-permute-start | bytes 110600 | tf_op jit(solution)/shard_map/ppermute | solution.py:167
  119.3 5.6 %collective-permute-start.21 = (bf16[24,768]{1,0:T(8,128)(2,1)S(1)}, bf16[24,768]{1,0:T(8,128)(2,1)S(1)}, u32[]{:S(2)}, u32[]{:S(2)}) collective-permute-start(bf16[24,768]{1,0:T(8,128)(2,1)S(1)} %get-tuple-element.60), channel_id=1, source_target_pairs={{0,8},{4,12},{8,0},{12,4},{16,24},{20,28},{24,16},{28,20},{1,9},{5... | collective-permute-start | bytes 110600 | tf_op jit(solution)/shard_map/ppermute | solution.py:167
  122.4 33.7 %collective-permute-start.44 = (bf16[2,768,768]{2,1,0:T(8,128)(2,1)S(1)}, bf16[2,768,768]{2,1,0:T(8,128)(2,1)S(1)}, u32[]{:S(2)}, u32[]{:S(2)}) collective-permute-start(bf16[2,768,768]{2,1,0:T(8,128)(2,1)S(1)} %dynamic-slice_bitcast_fusion), channel_id=1, source_target_pairs={{0,1},{1,0},{2,3},{3,2},{4,5},{5,4},{6,7},{7,6},{8,9},{9,8},{10,11... | collective-permute-start | bytes 7077896 | tf_op jit(solution)/shard_map/ppermute | solution.py:167
  124.3 102.4 %collective-permute-start.4 = (bf16[1,256,768]{2,1,0:T(8,128)(2,1)S(1)}, bf16[1,256,768]{2,1,0:T(8,128)(2,1)S(1)}, u32[]{:S(2)}, u32[]{:S(2)}) collective-permute-start(bf16[1,256,768]{2,1,0:T(8,128)(2,1)S(1)} %slice.78), channel_id=1, source_target_pairs={{0,2},{1,3},{2,0},{3,1},{4,6},{5,7},{6,4},{7,5},{8,10},{9,11},{10,... | collective-permute-start | bytes 1179656 | tf_op jit(solution)/shard_map/ppermute | solution.py:167
  125.1 31.0 %slice-start.2 = ((s8[4718592]{0:T(1024)(128)(4,1)}), s8[4194304]{0:T(1024)(128)(4,1)S(1)}, s32[]{:S(2)}) async-start(s8[4718592]{0:T(1024)(128)(4,1)} %bitcast.165), calls=%async_computation.2 | async-start | bytes 8388608
  125.2 30.9 %slice-start.3 = ((s8[4718592]{0:T(1024)(128)(4,1)}), s8[524288]{0:T(1024)(128)(4,1)S(1)}, s32[]{:S(2)}) async-start(s8[4718592]{0:T(1024)(128)(4,1)} %bitcast.165), calls=%async_computation.3 | async-start | bytes 1048576
  125.2 30.2 %collective-permute-start.6 = (bf16[1,192,2304]{2,1,0:T(8,128)(2,1)S(1)}, bf16[1,192,2304]{2,1,0:T(8,128)(2,1)S(1)}, u32[]{:S(2)}, u32[]{:S(2)}) collective-permute-start(bf16[1,192,2304]{2,1,0:T(8,128)(2,1)S(1)} %constant_dynamic-slice_fusion.3), channel_id=1, source_target_pairs={{0,2},{1,3},{2,0},{3,1},{4,6},{5,7},{6,4},{7,5},{8,10},{9,11},{10,... | collective-permute-start | bytes 2654216 | tf_op jit(solution)/shard_map/ppermute | solution.py:167
  127.1 53.5 %collective-permute-start.32 = (bf16[1,192,3072]{2,1,0:T(8,128)(2,1)S(1)}, bf16[1,192,3072]{2,1,0:T(8,128)(2,1)S(1)}, u32[]{:S(2)}, u32[]{:S(2)}) collective-permute-start(bf16[1,192,3072]{2,1,0:T(8,128)(2,1)S(1)} %constant_dynamic-slice_fusion.1), channel_id=1, source_target_pairs={{0,2},{1,3},{2,0},{3,1},{4,6},{5,7},{6,4},{7,5},{8,10},{9,11},{10,... | collective-permute-start | bytes 3538952 | tf_op jit(solution)/shard_map/ppermute | solution.py:167
  155.5 8.4 %collective-permute-start.7 = (bf16[96,2304]{1,0:T(8,128)(2,1)S(1)}, bf16[96,2304]{1,0:T(8,128)(2,1)S(1)}, u32[]{:S(2)}, u32[]{:S(2)}) collective-permute-start(bf16[96,2304]{1,0:T(8,128)(2,1)S(1)} %dynamic-slice_bitcast_fusion.6), channel_id=1, source_target_pairs={{0,4},{4,0},{8,12},{12,8},{16,20},{20,16},{24,28},{28,24},{1,5},{5... | collective-permute-start | bytes 1327112 | tf_op jit(solution)/shard_map/ppermute | solution.py:167
  156.4 47.1 %collective-permute-start.45 = (bf16[1,768,768]{2,1,0:T(8,128)(2,1)S(1)}, bf16[1,768,768]{2,1,0:T(8,128)(2,1)S(1)}, u32[]{:S(2)}, u32[]{:S(2)}) collective-permute-start(bf16[1,768,768]{2,1,0:T(8,128)(2,1)S(1)} %constant_dynamic-slice_fusion), channel_id=1, source_target_pairs={{0,2},{1,3},{2,0},{3,1},{4,6},{5,7},{6,4},{7,5},{8,10},{9,11},{10,... | collective-permute-start | bytes 3538952 | tf_op jit(solution)/shard_map/ppermute | solution.py:167
  164.0 17.2 %collective-permute-start.10 = (bf16[24,2304]{1,0:T(8,128)(2,1)S(1)}, bf16[24,2304]{1,0:T(8,128)(2,1)S(1)}, u32[]{:S(2)}, u32[]{:S(2)}) collective-permute-start(bf16[24,2304]{1,0:T(8,128)(2,1)S(1)} %get-tuple-element.58), channel_id=1, source_target_pairs={{0,24},{4,28},{8,16},{12,20},{16,8},{20,12},{24,0},{28,4},{1,25},{... | collective-permute-start | bytes 331784 | tf_op jit(solution)/shard_map/ppermute | solution.py:167
  166.8 15.0 %collective-permute-start.9 = (bf16[24,2304]{1,0:T(8,128)(2,1)S(1)}, bf16[24,2304]{1,0:T(8,128)(2,1)S(1)}, u32[]{:S(2)}, u32[]{:S(2)}) collective-permute-start(bf16[24,2304]{1,0:T(8,128)(2,1)S(1)} %get-tuple-element.59), channel_id=1, source_target_pairs={{0,16},{4,20},{8,24},{12,28},{16,0},{20,4},{24,8},{28,12},{1,17},{... | collective-permute-start | bytes 331784 | tf_op jit(solution)/shard_map/ppermute | solution.py:167
  180.6 4.7 %collective-permute-start.8 = (bf16[24,2304]{1,0:T(8,128)(2,1)S(1)}, bf16[24,2304]{1,0:T(8,128)(2,1)S(1)}, u32[]{:S(2)}, u32[]{:S(2)}) collective-permute-start(bf16[24,2304]{1,0:T(8,128)(2,1)S(1)} %get-tuple-element.57), channel_id=1, source_target_pairs={{0,8},{4,12},{8,0},{12,4},{16,24},{20,28},{24,16},{28,20},{1,9},{5... | collective-permute-start | bytes 331784 | tf_op jit(solution)/shard_map/ppermute | solution.py:167
  181.2 24.1 %collective-permute-start.24 = (bf16[24,768]{1,0:T(8,128)(2,1)S(1)}, bf16[24,768]{1,0:T(8,128)(2,1)S(1)}, u32[]{:S(2)}, u32[]{:S(2)}) collective-permute-start(bf16[24,768]{1,0:T(8,128)(2,1)S(1)} %fusion.38.refs_1_), channel_id=1, source_target_pairs={{0,4},{4,0},{8,12},{12,8},{16,20},{20,16},{24,28},{28,24},{1,5},{5... | collective-permute-start | bytes 110600 | tf_op jit(solution)/shard_map/ppermute | solution.py:167
  181.7 25.2 %collective-permute-start.25 = (bf16[24,768]{1,0:T(8,128)(2,1)S(1)}, bf16[24,768]{1,0:T(8,128)(2,1)S(1)}, u32[]{:S(2)}, u32[]{:S(2)}) collective-permute-start(bf16[24,768]{1,0:T(8,128)(2,1)S(1)} %fusion.38.refs_1_), channel_id=1, source_target_pairs={{0,8},{4,12},{8,0},{12,4},{16,24},{20,28},{24,16},{28,20},{1,9},{5... | collective-permute-start | bytes 110600 | tf_op jit(solution)/shard_map/ppermute | solution.py:167
  185.4 21.0 %collective-permute-start.33 = (bf16[96,3072]{1,0:T(8,128)(2,1)S(1)}, bf16[96,3072]{1,0:T(8,128)(2,1)S(1)}, u32[]{:S(2)}, u32[]{:S(2)}) collective-permute-start(bf16[96,3072]{1,0:T(8,128)(2,1)S(1)} %dynamic-slice_bitcast_fusion.4), channel_id=1, source_target_pairs={{0,4},{4,0},{8,12},{12,8},{16,20},{20,16},{24,28},{28,24},{1,5},{5... | collective-permute-start | bytes 1769480 | tf_op jit(solution)/shard_map/ppermute | solution.py:167
  203.5 5.1 %collective-permute-start.27 = (bf16[24,768]{1,0:T(8,128)(2,1)S(1)}, bf16[24,768]{1,0:T(8,128)(2,1)S(1)}, u32[]{:S(2)}, u32[]{:S(2)}) collective-permute-start(bf16[24,768]{1,0:T(8,128)(2,1)S(1)} %fusion.38.refs_1_), channel_id=1, source_target_pairs={{0,16},{4,20},{8,24},{12,28},{16,0},{20,4},{24,8},{28,12},{1,17},{... | collective-permute-start | bytes 110600 | tf_op jit(solution)/shard_map/ppermute | solution.py:167
  205.3 5.8 %collective-permute-start.29 = (bf16[24,768]{1,0:T(8,128)(2,1)S(1)}, bf16[24,768]{1,0:T(8,128)(2,1)S(1)}, u32[]{:S(2)}, u32[]{:S(2)}) collective-permute-start(bf16[24,768]{1,0:T(8,128)(2,1)S(1)} %fusion.38.refs_1_), channel_id=1, source_target_pairs={{0,24},{4,28},{8,16},{12,20},{16,8},{20,12},{24,0},{28,4},{1,25},{... | collective-permute-start | bytes 110600 | tf_op jit(solution)/shard_map/ppermute | solution.py:167
  206.4 20.3 %collective-permute-start.46 = (bf16[384,768]{1,0:T(8,128)(2,1)S(1)}, bf16[384,768]{1,0:T(8,128)(2,1)S(1)}, u32[]{:S(2)}, u32[]{:S(2)}) collective-permute-start(bf16[384,768]{1,0:T(8,128)(2,1)S(1)} %dynamic-slice_bitcast_fusion.3), channel_id=1, source_target_pairs={{0,4},{4,0},{8,12},{12,8},{16,20},{20,16},{24,28},{28,24},{1,5},{5... | collective-permute-start | bytes 1769480 | tf_op jit(solution)/shard_map/ppermute | solution.py:167
  207.0 15.3 %collective-permute-start.26 = (bf16[24,768]{1,0:T(8,128)(2,1)S(1)}, bf16[24,768]{1,0:T(8,128)(2,1)S(1)}, u32[]{:S(2)}, u32[]{:S(2)}) collective-permute-start(bf16[24,768]{1,0:T(8,128)(2,1)S(1)} %collective-permute-done.25.refs_3_), channel_id=1, source_target_pairs={{0,4},{4,0},{8,12},{12,8},{16,20},{20,16},{24,28},{28,24},{1,5},{5... | collective-permute-start | bytes 110600 | tf_op jit(solution)/shard_map/ppermute | solution.py:167
  208.6 14.4 %collective-permute-start.28 = (bf16[24,768]{1,0:T(8,128)(2,1)S(1)}, bf16[24,768]{1,0:T(8,128)(2,1)S(1)}, u32[]{:S(2)}, u32[]{:S(2)}) collective-permute-start(bf16[24,768]{1,0:T(8,128)(2,1)S(1)} %collective-permute-done.27.refs_5_), channel_id=1, source_target_pairs={{0,4},{4,0},{8,12},{12,8},{16,20},{20,16},{24,28},{28,24},{1,5},{5... | collective-permute-start | bytes 110600 | tf_op jit(solution)/shard_map/ppermute | solution.py:167
  211.2 12.7 %collective-permute-start.30 = (bf16[24,768]{1,0:T(8,128)(2,1)S(1)}, bf16[24,768]{1,0:T(8,128)(2,1)S(1)}, u32[]{:S(2)}, u32[]{:S(2)}) collective-permute-start(bf16[24,768]{1,0:T(8,128)(2,1)S(1)} %collective-permute-done.29.refs_7_), channel_id=1, source_target_pairs={{0,4},{4,0},{8,12},{12,8},{16,20},{20,16},{24,28},{28,24},{1,5},{5... | collective-permute-start | bytes 110600 | tf_op jit(solution)/shard_map/ppermute | solution.py:167
  222.3 6.1 %collective-permute-start.11 = (bf16[24,2304]{1,0:T(8,128)(2,1)S(1)}, bf16[24,2304]{1,0:T(8,128)(2,1)S(1)}, u32[]{:S(2)}, u32[]{:S(2)}) collective-permute-start(bf16[24,2304]{1,0:T(8,128)(2,1)S(1)} %fusion.35.refs_1_), channel_id=1, source_target_pairs={{0,4},{4,0},{8,12},{12,8},{16,20},{20,16},{24,28},{28,24},{1,5},{5... | collective-permute-start | bytes 331784 | tf_op jit(solution)/shard_map/ppermute | solution.py:167
  223.1 7.1 %collective-permute-start.12 = (bf16[24,2304]{1,0:T(8,128)(2,1)S(1)}, bf16[24,2304]{1,0:T(8,128)(2,1)S(1)}, u32[]{:S(2)}, u32[]{:S(2)}) collective-permute-start(bf16[24,2304]{1,0:T(8,128)(2,1)S(1)} %fusion.35.refs_1_), channel_id=1, source_target_pairs={{0,8},{4,12},{8,0},{12,4},{16,24},{20,28},{24,16},{28,20},{1,9},{5... | collective-permute-start | bytes 331784 | tf_op jit(solution)/shard_map/ppermute | solution.py:167
  223.9 23.0 %collective-permute-start.36 = (bf16[24,3072]{1,0:T(8,128)(2,1)S(1)}, bf16[24,3072]{1,0:T(8,128)(2,1)S(1)}, u32[]{:S(2)}, u32[]{:S(2)}) collective-permute-start(bf16[24,3072]{1,0:T(8,128)(2,1)S(1)} %get-tuple-element.55), channel_id=1, source_target_pairs={{0,24},{4,28},{8,16},{12,20},{16,8},{20,12},{24,0},{28,4},{1,25},{... | collective-permute-start | bytes 442376 | tf_op jit(solution)/shard_map/ppermute | solution.py:167
  226.7 23.0 %collective-permute-start.35 = (bf16[24,3072]{1,0:T(8,128)(2,1)S(1)}, bf16[24,3072]{1,0:T(8,128)(2,1)S(1)}, u32[]{:S(2)}, u32[]{:S(2)}) collective-permute-start(bf16[24,3072]{1,0:T(8,128)(2,1)S(1)} %get-tuple-element.56), channel_id=1, source_target_pairs={{0,16},{4,20},{8,24},{12,28},{16,0},{20,4},{24,8},{28,12},{1,17},{... | collective-permute-start | bytes 442376 | tf_op jit(solution)/shard_map/ppermute | solution.py:167
  226.7 23.0 %collective-permute-start.34 = (bf16[24,3072]{1,0:T(8,128)(2,1)S(1)}, bf16[24,3072]{1,0:T(8,128)(2,1)S(1)}, u32[]{:S(2)}, u32[]{:S(2)}) collective-permute-start(bf16[24,3072]{1,0:T(8,128)(2,1)S(1)} %get-tuple-element.54), channel_id=1, source_target_pairs={{0,8},{4,12},{8,0},{12,4},{16,24},{20,28},{24,16},{28,20},{1,9},{5... | collective-permute-start | bytes 442376 | tf_op jit(solution)/shard_map/ppermute | solution.py:167
  228.4 16.5 %collective-permute-start.14 = (bf16[24,2304]{1,0:T(8,128)(2,1)S(1)}, bf16[24,2304]{1,0:T(8,128)(2,1)S(1)}, u32[]{:S(2)}, u32[]{:S(2)}) collective-permute-start(bf16[24,2304]{1,0:T(8,128)(2,1)S(1)} %fusion.35.refs_1_), channel_id=1, source_target_pairs={{0,16},{4,20},{8,24},{12,28},{16,0},{20,4},{24,8},{28,12},{1,17},{... | collective-permute-start | bytes 331784 | tf_op jit(solution)/shard_map/ppermute | solution.py:167
  230.1 15.8 %collective-permute-start.16 = (bf16[24,2304]{1,0:T(8,128)(2,1)S(1)}, bf16[24,2304]{1,0:T(8,128)(2,1)S(1)}, u32[]{:S(2)}, u32[]{:S(2)}) collective-permute-start(bf16[24,2304]{1,0:T(8,128)(2,1)S(1)} %fusion.35.refs_1_), channel_id=1, source_target_pairs={{0,24},{4,28},{8,16},{12,20},{16,8},{20,12},{24,0},{28,4},{1,25},{... | collective-permute-start | bytes 331784 | tf_op jit(solution)/shard_map/ppermute | solution.py:167
  244.9 6.5 %collective-permute-start.13 = (bf16[24,2304]{1,0:T(8,128)(2,1)S(1)}, bf16[24,2304]{1,0:T(8,128)(2,1)S(1)}, u32[]{:S(2)}, u32[]{:S(2)}) collective-permute-start(bf16[24,2304]{1,0:T(8,128)(2,1)S(1)} %collective-permute-done.12.refs_3_), channel_id=1, source_target_pairs={{0,4},{4,0},{8,12},{12,8},{16,20},{20,16},{24,28},{28,24},{1,5},{5... | collective-permute-start | bytes 331784 | tf_op jit(solution)/shard_map/ppermute | solution.py:167
  245.9 6.6 %collective-permute-start.15 = (bf16[24,2304]{1,0:T(8,128)(2,1)S(1)}, bf16[24,2304]{1,0:T(8,128)(2,1)S(1)}, u32[]{:S(2)}, u32[]{:S(2)}) collective-permute-start(bf16[24,2304]{1,0:T(8,128)(2,1)S(1)} %collective-permute-done.14.refs_5_), channel_id=1, source_target_pairs={{0,4},{4,0},{8,12},{12,8},{16,20},{20,16},{24,28},{28,24},{1,5},{5... | collective-permute-start | bytes 331784 | tf_op jit(solution)/shard_map/ppermute | solution.py:167
  246.9 8.3 %collective-permute-start.49 = (bf16[96,768]{1,0:T(8,128)(2,1)S(1)}, bf16[96,768]{1,0:T(8,128)(2,1)S(1)}, u32[]{:S(2)}, u32[]{:S(2)}) collective-permute-start(bf16[96,768]{1,0:T(8,128)(2,1)S(1)} %get-tuple-element.52), channel_id=1, source_target_pairs={{0,24},{4,28},{8,16},{12,20},{16,8},{20,12},{24,0},{28,4},{1,25},{... | collective-permute-start | bytes 442376 | tf_op jit(solution)/shard_map/ppermute | solution.py:167
  249.7 11.1 %collective-permute-start.48 = (bf16[96,768]{1,0:T(8,128)(2,1)S(1)}, bf16[96,768]{1,0:T(8,128)(2,1)S(1)}, u32[]{:S(2)}, u32[]{:S(2)}) collective-permute-start(bf16[96,768]{1,0:T(8,128)(2,1)S(1)} %get-tuple-element.53), channel_id=1, source_target_pairs={{0,16},{4,20},{8,24},{12,28},{16,0},{20,4},{24,8},{28,12},{1,17},{... | collective-permute-start | bytes 442376 | tf_op jit(solution)/shard_map/ppermute | solution.py:167
  249.7 11.1 %collective-permute-start.47 = (bf16[96,768]{1,0:T(8,128)(2,1)S(1)}, bf16[96,768]{1,0:T(8,128)(2,1)S(1)}, u32[]{:S(2)}, u32[]{:S(2)}) collective-permute-start(bf16[96,768]{1,0:T(8,128)(2,1)S(1)} %get-tuple-element.51), channel_id=1, source_target_pairs={{0,8},{4,12},{8,0},{12,4},{16,24},{20,28},{24,16},{28,20},{1,9},{5... | collective-permute-start | bytes 442376 | tf_op jit(solution)/shard_map/ppermute | solution.py:167
  251.4 11.5 %collective-permute-start.17 = (bf16[24,2304]{1,0:T(8,128)(2,1)S(1)}, bf16[24,2304]{1,0:T(8,128)(2,1)S(1)}, u32[]{:S(2)}, u32[]{:S(2)}) collective-permute-start(bf16[24,2304]{1,0:T(8,128)(2,1)S(1)} %collective-permute-done.16.refs_7_), channel_id=1, source_target_pairs={{0,4},{4,0},{8,12},{12,8},{16,20},{20,16},{24,28},{28,24},{1,5},{5... | collective-permute-start | bytes 331784 | tf_op jit(solution)/shard_map/ppermute | solution.py:167
  252.5 11.9 %collective-permute-start.37 = (bf16[24,3072]{1,0:T(8,128)(2,1)S(1)}, bf16[24,3072]{1,0:T(8,128)(2,1)S(1)}, u32[]{:S(2)}, u32[]{:S(2)}) collective-permute-start(bf16[24,3072]{1,0:T(8,128)(2,1)S(1)} %fusion.32.refs_1_), channel_id=1, source_target_pairs={{0,4},{4,0},{8,12},{12,8},{16,20},{20,16},{24,28},{28,24},{1,5},{5... | collective-permute-start | bytes 442376 | tf_op jit(solution)/shard_map/ppermute | solution.py:167
  255.2 10.2 %collective-permute-start.38 = (bf16[24,3072]{1,0:T(8,128)(2,1)S(1)}, bf16[24,3072]{1,0:T(8,128)(2,1)S(1)}, u32[]{:S(2)}, u32[]{:S(2)}) collective-permute-start(bf16[24,3072]{1,0:T(8,128)(2,1)S(1)} %fusion.32.refs_1_), channel_id=1, source_target_pairs={{0,8},{4,12},{8,0},{12,4},{16,24},{20,28},{24,16},{28,20},{1,9},{5... | collective-permute-start | bytes 442376 | tf_op jit(solution)/shard_map/ppermute | solution.py:167
  260.8 13.1 %collective-permute-start.40 = (bf16[24,3072]{1,0:T(8,128)(2,1)S(1)}, bf16[24,3072]{1,0:T(8,128)(2,1)S(1)}, u32[]{:S(2)}, u32[]{:S(2)}) collective-permute-start(bf16[24,3072]{1,0:T(8,128)(2,1)S(1)} %fusion.32.refs_1_), channel_id=1, source_target_pairs={{0,16},{4,20},{8,24},{12,28},{16,0},{20,4},{24,8},{28,12},{1,17},{... | collective-permute-start | bytes 442376 | tf_op jit(solution)/shard_map/ppermute | solution.py:167
  260.8 15.0 %collective-permute-start.42 = (bf16[24,3072]{1,0:T(8,128)(2,1)S(1)}, bf16[24,3072]{1,0:T(8,128)(2,1)S(1)}, u32[]{:S(2)}, u32[]{:S(2)}) collective-permute-start(bf16[24,3072]{1,0:T(8,128)(2,1)S(1)} %fusion.32.refs_1_), channel_id=1, source_target_pairs={{0,24},{4,28},{8,16},{12,20},{16,8},{20,12},{24,0},{28,4},{1,25},{... | collective-permute-start | bytes 442376 | tf_op jit(solution)/shard_map/ppermute | solution.py:167
  262.9 15.1 %collective-permute-start.51 = (bf16[96,768]{1,0:T(8,128)(2,1)S(1)}, bf16[96,768]{1,0:T(8,128)(2,1)S(1)}, u32[]{:S(2)}, u32[]{:S(2)}) collective-permute-start(bf16[96,768]{1,0:T(8,128)(2,1)S(1)} %fusion.29.refs_1_), channel_id=1, source_target_pairs={{0,8},{4,12},{8,0},{12,4},{16,24},{20,28},{24,16},{28,20},{1,9},{5... | collective-permute-start | bytes 442376 | tf_op jit(solution)/shard_map/ppermute | solution.py:167
  264.4 21.5 %collective-permute-start.53 = (bf16[96,768]{1,0:T(8,128)(2,1)S(1)}, bf16[96,768]{1,0:T(8,128)(2,1)S(1)}, u32[]{:S(2)}, u32[]{:S(2)}) collective-permute-start(bf16[96,768]{1,0:T(8,128)(2,1)S(1)} %fusion.29.refs_1_), channel_id=1, source_target_pairs={{0,16},{4,20},{8,24},{12,28},{16,0},{20,4},{24,8},{28,12},{1,17},{... | collective-permute-start | bytes 442376 | tf_op jit(solution)/shard_map/ppermute | solution.py:167
  265.4 21.7 %collective-permute-start.55 = (bf16[96,768]{1,0:T(8,128)(2,1)S(1)}, bf16[96,768]{1,0:T(8,128)(2,1)S(1)}, u32[]{:S(2)}, u32[]{:S(2)}) collective-permute-start(bf16[96,768]{1,0:T(8,128)(2,1)S(1)} %fusion.29.refs_1_), channel_id=1, source_target_pairs={{0,24},{4,28},{8,16},{12,20},{16,8},{20,12},{24,0},{28,4},{1,25},{... | collective-permute-start | bytes 442376 | tf_op jit(solution)/shard_map/ppermute | solution.py:167
  273.9 14.1 %collective-permute-start.39 = (bf16[24,3072]{1,0:T(8,128)(2,1)S(1)}, bf16[24,3072]{1,0:T(8,128)(2,1)S(1)}, u32[]{:S(2)}, u32[]{:S(2)}) collective-permute-start(bf16[24,3072]{1,0:T(8,128)(2,1)S(1)} %collective-permute-done.38.refs_3_), channel_id=1, source_target_pairs={{0,4},{4,0},{8,12},{12,8},{16,20},{20,16},{24,28},{28,24},{1,5},{5... | collective-permute-start | bytes 442376 | tf_op jit(solution)/shard_map/ppermute | solution.py:167
  275.8 13.3 %collective-permute-start.41 = (bf16[24,3072]{1,0:T(8,128)(2,1)S(1)}, bf16[24,3072]{1,0:T(8,128)(2,1)S(1)}, u32[]{:S(2)}, u32[]{:S(2)}) collective-permute-start(bf16[24,3072]{1,0:T(8,128)(2,1)S(1)} %collective-permute-done.40.refs_5_), channel_id=1, source_target_pairs={{0,4},{4,0},{8,12},{12,8},{16,20},{20,16},{24,28},{28,24},{1,5},{5... | collective-permute-start | bytes 442376 | tf_op jit(solution)/shard_map/ppermute | solution.py:167
  278.0 17.1 %collective-permute-start.50 = (bf16[96,768]{1,0:T(8,128)(2,1)S(1)}, bf16[96,768]{1,0:T(8,128)(2,1)S(1)}, u32[]{:S(2)}, u32[]{:S(2)}) collective-permute-start(bf16[96,768]{1,0:T(8,128)(2,1)S(1)} %fusion.29.refs_1_), channel_id=1, source_target_pairs={{0,4},{4,0},{8,12},{12,8},{16,20},{20,16},{24,28},{28,24},{1,5},{5... | collective-permute-start | bytes 442376 | tf_op jit(solution)/shard_map/ppermute | solution.py:167
  286.0 6.9 %collective-permute-start.43 = (bf16[24,3072]{1,0:T(8,128)(2,1)S(1)}, bf16[24,3072]{1,0:T(8,128)(2,1)S(1)}, u32[]{:S(2)}, u32[]{:S(2)}) collective-permute-start(bf16[24,3072]{1,0:T(8,128)(2,1)S(1)} %collective-permute-done.42.refs_7_), channel_id=1, source_target_pairs={{0,4},{4,0},{8,12},{12,8},{16,20},{20,16},{24,28},{28,24},{1,5},{5... | collective-permute-start | bytes 442376 | tf_op jit(solution)/shard_map/ppermute | solution.py:167
  287.1 8.9 %collective-permute-start.52 = (bf16[96,768]{1,0:T(8,128)(2,1)S(1)}, bf16[96,768]{1,0:T(8,128)(2,1)S(1)}, u32[]{:S(2)}, u32[]{:S(2)}) collective-permute-start(bf16[96,768]{1,0:T(8,128)(2,1)S(1)} %collective-permute-done.51.refs_3_), channel_id=1, source_target_pairs={{0,4},{4,0},{8,12},{12,8},{16,20},{20,16},{24,28},{28,24},{1,5},{5... | collective-permute-start | bytes 442376 | tf_op jit(solution)/shard_map/ppermute | solution.py:167
  288.0 11.1 %collective-permute-start.54 = (bf16[96,768]{1,0:T(8,128)(2,1)S(1)}, bf16[96,768]{1,0:T(8,128)(2,1)S(1)}, u32[]{:S(2)}, u32[]{:S(2)}) collective-permute-start(bf16[96,768]{1,0:T(8,128)(2,1)S(1)} %collective-permute-done.53.refs_5_), channel_id=1, source_target_pairs={{0,4},{4,0},{8,12},{12,8},{16,20},{20,16},{24,28},{28,24},{1,5},{5... | collective-permute-start | bytes 442376 | tf_op jit(solution)/shard_map/ppermute | solution.py:167
  289.1 11.6 %collective-permute-start.56 = (bf16[96,768]{1,0:T(8,128)(2,1)S(1)}, bf16[96,768]{1,0:T(8,128)(2,1)S(1)}, u32[]{:S(2)}, u32[]{:S(2)}) collective-permute-start(bf16[96,768]{1,0:T(8,128)(2,1)S(1)} %collective-permute-done.55.refs_7_), channel_id=1, source_target_pairs={{0,4},{4,0},{8,12},{12,8},{16,20},{20,16},{24,28},{28,24},{1,5},{5... | collective-permute-start | bytes 442376 | tf_op jit(solution)/shard_map/ppermute | solution.py:167
  (25 other events, 206.4 us)

commit v2 on v1

--- a/solution.py
+++ b/solution.py
@@ -162,83 +162,224 @@
     )(query, key, value, bias, grad, lse)
 
 
+LANES = 384
+QUARTERS = 4
+
+
+def quarter_slot(quarter):
+    return 2 * (quarter % 2) + quarter // 2
+
+
+def half_share_kernel(place_ref, *refs, plan, low):
+    keep_ref, send_ref, stage, turned = refs[4 * len(plan) :]
+    top, low_own, x_own, z_own = (place_ref[i] for i in range(4))
+    offset = 0
+    for index, (rows, cols) in enumerate(plan):
+        sides = (refs[4 * index : 4 * index + 2], refs[4 * index + 2 : 4 * index + 4])
+        half = rows // 2
+        share = half // low
+        strip = min(half, LANES)
+        piece_rows = share // QUARTERS
+        for start in range(0, half, strip):
+            lanes = pl.ds(pl.multiple_of(top * half + start, 128), strip)
+            for side, (left, _) in enumerate(sides):
+                turned[0:strip, side * T_DEV : (side + 1) * T_DEV] = left[:, lanes].T
+            for block in range(cols // D):
+                grad = sum(
+                    dot(
+                        turned[0:strip, side * T_DEV : (side + 1) * T_DEV],
+                        right[:, block * D : (block + 1) * D],
+                    )
+                    for side, (_, right) in enumerate(sides)
+                )
+                for part in range(D // LANES):
+                    column = block * D + part * LANES
+                    side_x = column // (cols // 2)
+                    slot = offset + (column % (cols // 2)) // LANES * piece_rows
+                    for row in range(0, strip, piece_rows):
+                        at = start + row
+                        low_other = at // share
+                        quarter = at % share // piece_rows
+                        stage[
+                            low_other ^ low_own,
+                            side_x ^ x_own,
+                            quarter_slot(quarter ^ z_own),
+                            slot : slot + piece_rows,
+                            :,
+                        ] = grad[
+                            row : row + piece_rows, part * LANES : (part + 1) * LANES
+                        ].astype(BF16)
+        offset += piece_rows * (cols // 2 // LANES)
+    keep_ref[...] = stage[0 : low // 2]
+    send_ref[...] = stage[low // 2 : low]
+
+
+VMEM_SPEC = pl.BlockSpec(memory_space=pltpu.VMEM)
+SMEM_SPEC = pl.BlockSpec(memory_space=pltpu.SMEM)
+
+
+def half_share_grads(place, weights, n_seq, name):
+    low = n_seq // 2
+    plan = [(w[0].shape[1], w[1].shape[1]) for w in weights]
+    piece_rows = sum(r // n_seq // QUARTERS * (c // 2 // LANES) for r, c in plan)
+    shape = (2, QUARTERS, piece_rows, LANES)
+    return pl.pallas_call(
+        lambda *refs: half_share_kernel(*refs, plan=plan, low=low),
+        in_specs=[SMEM_SPEC] + [VMEM_SPEC] * (4 * len(weights)),
+        out_specs=[VMEM_SPEC] * 2,
+        out_shape=[jax.ShapeDtypeStruct((low // 2, *shape), BF16)] * 2,
+        scratch_shapes=[pltpu.VMEM((low, *shape), BF16), pltpu.VMEM((LANES, 2 * T_DEV), BF16)],
+        compiler_params=pltpu.CompilerParams(vmem_limit_bytes=48 * MIB),
+        name=name,
+    )(place, *[array for weight in weights for array in weight])
+
+
+def full_share_kernel(place_ref, group_ref, dq_ref, dk_ref, dv_ref, keep_ref, send_ref, stage, turned, *, n_seq):
+    top, low_own, x_own, z_own = (place_ref[i] for i in range(4))
+    seq_own = top * (n_seq // 2) + low_own
+    share = D // n_seq
+    piece_rows = share // QUARTERS
+    tokens = group_ref.shape[0]
+    for start in range(0, D, LANES):
+        turned[...] = group_ref[:, start : start + LANES].T
+        for index, right in enumerate((dq_ref, dk_ref, dv_ref)):
+            if index == 0:
+                grad = dot(turned[:, 0:T_DEV], right[...]) * 0.125
+            else:
+                grad = dot(turned[...], right[...])
+            for part in range(D // LANES):
+                for row in range(0, LANES, piece_rows):
+                    at = start + row
+                    relative = (at // share) ^ seq_own
+                    stage[
+                        relative % 2 * (n_seq // 2) + relative // 2,
+                        part ^ x_own,
+                        quarter_slot(at % share // piece_rows ^ z_own),
+                        index * piece_rows : (index + 1) * piece_rows,
+                        :,
+                    ] = grad[row : row + piece_rows, part * LANES : (part + 1) * LANES].astype(BF16)
+    keep_ref[...] = stage[0 : n_seq // 2]
+    send_ref[...] = stage[n_seq // 2 : n_seq]
+
+
+def full_share_grads(place, group, d_query, d_key, d_value, n_seq):
+    piece_rows = 3 * (D // n_seq // QUARTERS)
+    shape = (2, QUARTERS, piece_rows, LANES)
+    return pl.pallas_call(
+        lambda *refs: full_share_kernel(*refs, n_seq=n_seq),
+        in_specs=[SMEM_SPEC] + [VMEM_SPEC] * 4,
+        out_specs=[VMEM_SPEC] * 2,
+        out_shape=[jax.ShapeDtypeStruct((n_seq // 2, *shape), BF16)] * 2,
+        scratch_shapes=[
+            pltpu.VMEM((n_seq, *shape), BF16),
+            pltpu.VMEM((LANES, group.shape[0]), BF16),
+        ],
+        compiler_params=pltpu.CompilerParams(vmem_limit_bytes=48 * MIB),
+        name="grads_qkv",
+    )(place, group, d_query, d_key, d_value)
+
+
+def assemble_kernel(place_ref, *refs, plan):
+    outs = refs[len(refs) - len(plan) :]
+    x_own, z_own = place_ref[2], place_ref[3]
+    index = 0
+    for ref in refs[: len(refs) - len(plan)]:
+        for slot in range(ref.shape[0]):
+            relative, column = index % QUARTERS, index // QUARTERS
+            quarter = (relative // 2 + relative % 2 * 2) ^ z_own
+            offset = 0
+            for out, (rows, cols) in zip(outs, plan):
+                height = rows // QUARTERS
+                at = pl.ds(pl.multiple_of(quarter * height, 8), height)
+                for part in range(cols // 2 // LANES):
+                    lanes = pl.ds(
+                        pl.multiple_of((column ^ x_own) * (cols // 2) + part * LANES, 128), LANES
+                    )
+                    out[at, lanes] = ref[slot, offset : offset + height, :].astype(F32)
+                    offset += height
+            index += 1
+
+
+def assemble(place, pieces, plan, name):
+    return pl.pallas_call(
+        lambda *refs: assemble_kernel(*refs, plan=plan),
+        in_specs=[SMEM_SPEC] + [VMEM_SPEC] * len(pieces),
+        out_specs=[VMEM_SPEC] * len(plan),
+        out_shape=[jax.ShapeDtypeStruct(shape, F32) for shape in plan],
+        compiler_params=pltpu.CompilerParams(vmem_limit_bytes=32 * MIB),
+        name=name,
+    )(place, *pieces)
+
+
 def swap(value, axis, mask):
     size = lax.axis_size(axis)
     return lax.ppermute(value, axis, [(i, i ^ mask) for i in range(size)])
 
 
-def pick(value, index):
-    return lax.dynamic_index_in_dim(value, index, 0, keepdims=False)
-
-
-def reduce_pieces(grad):
-    n_seq, n_dp = lax.axis_size("seq"), lax.axis_size("dp")
-    seq, dp = lax.axis_index("seq"), lax.axis_index("dp")
-    cols = grad.shape[1]
-    share = grad.shape[0] // n_seq
-    core = seq % 2
-    halves = jnp.swapaxes(grad.reshape(n_seq // 2, 2, share, cols), 0, 1)
-    total = pick(halves, core) + swap(pick(halves, 1 - core), "seq", 1)
-    step = n_seq // 2
-    while step > 1:
-        step //= 2
-        bit = (seq // (2 * step)) % 2
-        halves = total.reshape(2, step, share, cols)
-        total = pick(halves, bit) + swap(pick(halves, 1 - bit), "seq", 2 * step)
-    bit = dp % 2
-    halves = total.reshape(2, share // 2, cols)
-    total = pick(halves, bit) + swap(pick(halves, 1 - bit), "dp", 1)
-    rest = n_dp // 2
-    blocks = total.reshape(rest, share // n_dp, cols)
-    place = dp // 2
-    piece = pick(blocks, place).astype(F32)
-    for other in range(1, rest):
-        piece = piece + swap(pick(blocks, place ^ other), "dp", 2 * other).astype(F32)
-    return piece.astype(BF16)
-
-
-def gather_pieces(piece):
-    rest = lax.axis_size("dp") // 2
-    pieces = [None] * (2 * rest)
-    for other in range(rest):
-        pieces[2 * other] = piece if other == 0 else swap(piece, "dp", 2 * other)
-    for other in range(rest):
-        pieces[2 * other + 1] = swap(pieces[2 * other], "dp", 1)
-    return pieces
-
-
-def assemble_kernel(place_ref, *refs, widths):
-    outs = refs[len(refs) - len(widths) :]
-    for piece_ref, index in zip(refs, range(len(refs) - len(widths))):
-        rows = piece_ref.shape[0]
-        start = pl.multiple_of(place_ref[index] * rows, 8)
-        offset = 0
-        for out_ref, width in zip(outs, widths):
-            out_ref[pl.ds(start, rows), :] = piece_ref[:, offset : offset + width].astype(F32)
-            offset += width
-
-
-def assemble(pieces, widths):
-    n_dp = len(pieces)
-    dp = lax.axis_index("dp") ^ jnp.arange(n_dp, dtype=jnp.int32)
-    places = dp % 2 * (n_dp // 2) + dp // 2
-    rows, cols = pieces[0].shape
-    if rows % 8:
-        stacked = jnp.zeros((n_dp, rows, cols), F32)
-        for i, piece in enumerate(pieces):
-            stacked = lax.dynamic_update_slice(stacked, piece.astype(F32)[None], (places[i], 0, 0))
-        full = stacked.reshape(n_dp * rows, cols)
-        cuts = [sum(widths[:i]) for i in range(len(widths))]
-        return [full[:, c : c + w] for c, w in zip(cuts, widths)]
-    return pl.pallas_call(
-        lambda *refs: assemble_kernel(*refs, widths=widths),
-        in_specs=[pl.BlockSpec(memory_space=pltpu.SMEM)]
-        + [pl.BlockSpec(memory_space=pltpu.VMEM)] * n_dp,
-        out_specs=[pl.BlockSpec(memory_space=pltpu.VMEM)] * len(widths),
-        out_shape=[jax.ShapeDtypeStruct((n_dp * rows, w), F32) for w in widths],
-        compiler_params=pltpu.CompilerParams(vmem_limit_bytes=24 * MIB),
-        name="assemble",
-    )(places, *pieces)
+def summed(terms):
+    total = terms[0].astype(F32)
+    for term in terms[1:]:
+        total = total + term.astype(F32)
+    return total.astype(BF16)
+
+
+def halve(terms, axis, mask):
+    half = terms[0].shape[0] // 2
+    got = swap(summed([t[half:] for t in terms]), axis, mask)
+    return [t[:half] for t in terms] + [got]
+
+
+def reduce_and_gather(keep, send, seq_masks):
+    n_dp = lax.axis_size("dp")
+    terms = [keep, swap(send, "seq", seq_masks[0])]
+    for mask in seq_masks[1:]:
+        terms = halve(terms, "seq", mask)
+    terms = halve([t[0] for t in terms], "dp", 1)
+    terms = halve([t[0] for t in terms], "dp", 2)
+    terms = halve(terms, "dp", 4)
+    piece = summed(terms)
+    step = 8
+    while step < n_dp:
+        piece = summed([piece, swap(piece, "dp", step)])
+        step *= 2
+    second = swap(piece, "dp", 4)
+    pair = jnp.concatenate([piece, second])
+    others = swap(pair, "dp", 2)
+    return [piece, second, others, swap(jnp.concatenate([pair, others]), "dp", 1)]
+
+
+def after_attention(tokens, mixed, out_grad, weights):
+    w_proj, proj_bias, gain1, bias1, w_up, up_bias, w_down, down_bias, gain2, bias2 = weights
+    resid_one = tokens.astype(F32) + dot(mixed, w_proj) + proj_bias
+    normed, ln1_pull = jax.vjp(layer_norm, resid_one, gain1, bias1)
+    normed_low = normed.astype(BF16)
+    hidden_pre = dot(normed_low, w_up) + up_bias
+    activated, gelu_pull = jax.vjp(gelu_tanh, hidden_pre)
+    hidden = activated.astype(BF16)
+    branch = dot(hidden, w_down) + down_bias
+    final_out, ln2_pull = jax.vjp(layer_norm, normed + branch, gain2, bias2)
+    d_resid2, d_gain2, d_bias2 = ln2_pull(out_grad.astype(F32))
+    d_branch = d_resid2.astype(BF16)
+    d_hidden = dot(d_branch, w_down, NT).astype(BF16)
+    (d_pre_raw,) = gelu_pull(d_hidden.astype(F32))
+    d_pre = d_pre_raw.astype(BF16)
+    d_normed = d_resid2 + dot(d_pre, w_up, NT)
+    d_resid1, d_gain1, d_bias1 = ln1_pull(d_normed)
+    d_attn = d_resid1.astype(BF16)
+    return dict(
+        layer_out=final_out.astype(BF16),
+        normed_low=normed_low,
+        hidden=hidden,
+        d_branch=d_branch,
+        d_pre=d_pre,
+        d_attn=d_attn,
+        d_resid1=d_resid1,
+        small=(d_gain1, d_bias1, d_gain2, d_bias2),
+    )
+
+
+def column_sum(array):
+    return jnp.sum(array.astype(F32), axis=0)
 
 
 def on_device(
@@ -263,10 +404,13 @@
     out_grad,
 ):
     n_seq, n_dp = lax.axis_size("seq"), lax.axis_size("dp")
-    device = lax.axis_index("seq")
+    device, dp = lax.axis_index("seq"), lax.axis_index("dp")
+    low = n_seq // 2
+    place = jnp.stack([device // low, device % low, dp % 2, dp // 2 % QUARTERS]).astype(jnp.int32)
     tok_rows = inputs.reshape(T_DEV, D)
+    cotangent = out_grad.reshape(T_DEV, D)
     parts = [tok_rows] + [None] * (n_seq - 1)
-    step = n_seq // 2
+    step = low
     while step > 1:
         for j in range(0, n_seq, 2 * step):
             parts[j + step] = swap(parts[j], "seq", step)
@@ -274,6 +418,7 @@
     for j in range(0, n_seq, 2):
         parts[j + 1] = swap(parts[j], "seq", 1)
     tok_group = jnp.concatenate(parts)
+    cotangent_partner = swap(cotangent, "seq", low)
     bias = block_bias(device, random_blocks[0], long_group[0] == 1, n_seq)
     bias = jnp.repeat(bias, BLOCK, axis=1)
 
@@ -281,68 +426,68 @@
     key = dot(tok_group, w_key).astype(BF16)
     value = (dot(tok_group, w_value) + value_bias).astype(BF16)
     mixed, lse = attn_fwd(query, key, value, bias)
-    attn_out = dot(mixed, w_proj) + proj_bias
-    resid_one = tok_rows.astype(F32) + attn_out
-    normed, ln1_pull = jax.vjp(
-        layer_norm, resid_one, ln1_gain.astype(F32), ln1_bias.astype(F32)
-    )
-    normed_low = normed.astype(BF16)
-    hidden_pre = dot(normed_low, w_up) + up_bias
-    activated, gelu_pull = jax.vjp(gelu_tanh, hidden_pre)
-    hidden = activated.astype(BF16)
-    branch = dot(hidden, w_down) + down_bias
-    final_out, ln2_pull = jax.vjp(
-        layer_norm, normed + branch, ln2_gain.astype(F32), ln2_bias.astype(F32)
-    )
-    layer_out = final_out.astype(BF16).reshape(1, T_DEV, D)
-    d_resid2, d_gain2, d_bias2 = ln2_pull(out_grad.reshape(T_DEV, D).astype(F32))
-    d_branch = d_resid2.astype(BF16)
-    piece_down = reduce_pieces(dot(hidden, d_branch, TN).astype(BF16))
-    grad_down_b = jnp.sum(d_branch.astype(F32), axis=0)
-    d_hidden = dot(d_branch, w_down, NT).astype(BF16)
-    (d_pre_raw,) = gelu_pull(d_hidden.astype(F32))
-    d_pre = d_pre_raw.astype(BF16)
-    piece_up = reduce_pieces(dot(normed_low, d_pre, TN).astype(BF16))
-    grad_up_b = jnp.sum(d_pre.astype(F32), axis=0)
-    d_normed = d_resid2 + dot(d_pre, w_up, NT)
-    d_resid1, d_gain1, d_bias1 = ln1_pull(d_normed)
-    d_attn = d_resid1.astype(BF16)
-    piece_proj = reduce_pieces(dot(mixed, d_attn, TN).astype(BF16))
-    grad_proj_b = jnp.sum(d_attn.astype(F32), axis=0)
-    d_mixed = dot(d_attn, w_proj, NT).astype(BF16)
-
+    mixed_partner = swap(mixed, "seq", low)
+    weights = (
+        w_proj,
+        proj_bias,
+        ln1_gain.astype(F32),
+        ln1_bias.astype(F32),
+        w_up,
+        up_bias,
+        w_down,
+        down_bias,
+        ln2_gain.astype(F32),
+        ln2_bias.astype(F32),
+    )
+    own = after_attention(tok_rows, mixed, cotangent, weights)
+    other = after_attention(parts[low], mixed_partner, cotangent_partner, weights)
+    down_terms = half_share_grads(
+        place,
+        [(own["hidden"], own["d_branch"], other["hidden"], other["d_branch"])],
+        n_seq,
+        "grads_down",
+    )
+    up_terms = half_share_grads(
+        place,
+        [
+            (own["normed_low"], own["d_pre"], other["normed_low"], other["d_pre"]),
+            (mixed, own["d_attn"], mixed_partner, other["d_attn"]),
+        ],
+        n_seq,
+        "grads_up_proj",
+    )
+    low_masks = [1 << i for i in reversed(range(n_seq.bit_length() - 2))]
+    pieces_down = reduce_and_gather(*down_terms, low_masks)
+    pieces_up = reduce_and_gather(*up_terms, low_masks)
+
+    d_mixed = dot(own["d_attn"], w_proj, NT).astype(BF16)
     d_query, d_key, d_value = attn_bwd(query, key, value, bias, d_mixed, lse)
-    piece_qkv = reduce_pieces(
-        jnp.concatenate(
-            [
-                (dot(tok_rows, d_query, TN) * 0.125).astype(BF16),
-                dot(tok_group, d_key, TN).astype(BF16),
-                dot(tok_group, d_value, TN).astype(BF16),
-            ],
-            axis=1,
-        )
-    )
-    grad_query_b = jnp.sum(d_query.astype(F32), axis=0) * 0.125
-    grad_value_b = jnp.sum(d_value.astype(F32), axis=0)
+    qkv_terms = full_share_grads(place, tok_group, d_query, d_key, d_value, n_seq)
+    pieces_qkv = reduce_and_gather(
+        *qkv_terms, [1] + [1 << i for i in reversed(range(1, n_seq.bit_length() - 1))]
+    )
 
     term = (dot(d_key, w_key, NT) + dot(d_value, w_value, NT)).astype(BF16)
-    term = term.reshape(n_seq // 2, 2, T_DEV, D)
-    total = term[:, 0].astype(F32) + swap(term[:, 1], "seq", 1).astype(F32)
-    step = n_seq // 2
+    term = term.reshape(low, 2, T_DEV, D)
+    total = [term[:, 0], swap(term[:, 1], "seq", 1)]
+    step = low
     while step > 1:
         step //= 2
-        total = total[:step] + swap(total[step:].astype(BF16), "seq", 2 * step).astype(F32)
-    input_grad = d_resid1 + 0.125 * dot(d_query, w_query, NT) + total[0]
-
+        total = halve(total, "seq", 2 * step)
+    input_grad = own["d_resid1"] + 0.125 * dot(d_query, w_query, NT)
+    for part in total:
+        input_grad = input_grad + part[0].astype(F32)
+
+    d_gain1, d_bias1, d_gain2, d_bias2 = own["small"]
     small = jnp.concatenate(
         [
-            grad_query_b,
-            grad_value_b,
-            grad_proj_b,
+            column_sum(d_query) * 0.125,
+            column_sum(d_value),
+            column_sum(own["d_attn"]),
             d_gain1,
             d_bias1,
-            grad_up_b,
-            grad_down_b,
+            column_sum(own["d_pre"]),
+            column_sum(own["d_branch"]),
             d_gain2,
             d_bias2,
         ]
@@ -353,13 +498,13 @@
             small = small + swap(small, axis, step)
             step *= 2
 
-    (grad_down,) = assemble(gather_pieces(piece_down), [D])
-    (grad_up,) = assemble(gather_pieces(piece_up), [FF])
-    (grad_proj,) = assemble(gather_pieces(piece_proj), [D])
-    grad_query, grad_key, grad_value = assemble(gather_pieces(piece_qkv), [D, D, D])
+    square = (D // n_seq, D)
+    (grad_down,) = assemble(place, pieces_down, [(FF // n_seq, D)], "assemble_down")
+    grad_up, grad_proj = assemble(place, pieces_up, [(D // n_seq, FF), square], "assemble_up")
+    grad_query, grad_key, grad_value = assemble(place, pieces_qkv, [square] * 3, "assemble_qkv")
     up_end = 5 * D + FF
     return (
-        layer_out,
+        own["layer_out"].reshape(1, T_DEV, D),
         input_grad.reshape(1, T_DEV, D),
         grad_query,
         grad_key,

time: 304 us -> 242 us (0.80)
  waiting for transfers between devices: 128 us -> 88.1 us
  starting transfers between devices: 72 us -> 44.9 us
  local copies, waits for them, and re-layouts: 16.4 us -> 4.25 us
  Pallas kernels: 31.4 us -> 43 us
  other arithmetic: 17.6 us -> 25.5 us
  matrix products: 34.8 us -> 29.7 us
    ppermute x62 -> x34, waiting for transfers between devices: 128 us -> 88.1 us  [swap(): return lax.ppermute(value, axis, [(i, i ^ mask) for i in range(size)])]
    ppermute x62 -> x34, starting transfers between devices: 72 us -> 44.9 us  [swap(): return lax.ppermute(value, axis, [(i, i ^ mask) for i in range(size)])]
    pallas_call x4 -> x6, Pallas kernels: 7.46 us -> 19 us  [the longest x2 7.18 us: half_share_grads(): pl.pallas_call(lambda *refs: half_share_kernel(*refs, plan=plan, low=low)...]
    convert_element_type x7 -> x20, other arithmetic: 2.31 us -> 11 us  [the longest x14 6.65 us: summed(): return total.astype(BF16)]
    squeeze x17 -> x1, local copies, waits for them, and re-layouts: 7.7 us -> 0.05 us  [on_device(): total = [term[:, 0], swap(term[:, 1], 'seq', 1)]]
    concatenate x2 -> x1, local copies, waits for them, and re-layouts: 5.81 us -> 0.01 us  [on_device(): jnp.concatenate([column_sum(d_query) * 0.125, column_sum(d_value), column...]
    dot_general x18 -> x17, matrix products: 34.8 us -> 29.7 us  [dot(): return lax.dot_general(left, right, dims, preferred_element_type=F32)]
    add x14 -> x0, other arithmetic: 3.71 us -> none  [the longest x4 1.8 us: reduce_pieces(): total = pick(halves, core) + swap(pick(halves, 1 - core), 'seq', 1)]
  transfers between devices with their start and end apart: 62 -> 34, of which waited for: 21 -> 18; matrix products, arithmetic and copies ran while one was open for 12% -> 17% of each run, Pallas kernels for 2% -> 8%
where the time goes in v2:
time: 242 us; the launch traced here: 238 us
  waiting for transfers between devices  88.1 us (36%)
  starting transfers between devices  44.9 us (19%)
  Pallas kernels  43 us (18%)
  matrix products  29.7 us (12%)
  other arithmetic  25.5 us (11%)
  local copies, waits for them, and re-layouts  4.25 us (2%)
  between operations  2.61 us (1%)
    ppermute x34, waiting for transfers between devices, swap(): return lax.ppermute(value, axis, [(i, i ^ mask) for i in range(size)])  88.1 us
    ppermute x34, starting transfers between devices, swap(): return lax.ppermute(value, axis, [(i, i ^ mask) for i in range(size)])  44.9 us
    dot_general x17, matrix products, dot(): return lax.dot_general(left, right, dims, preferred_element_type=F32)  29.7 us
    pallas_call x1, Pallas kernels, attn_bwd(): pl.pallas_call(attn_bwd_kernel, grid=(HEADS // 2,), in_specs=[head_pair(r...  14.5 us
    pallas_call x1, Pallas kernels, attn_fwd(): pl.pallas_call(attn_fwd_kernel, grid=(HEADS // 2,), in_specs=[head_pair(r...  9.46 us
    pallas_call x2, Pallas kernels, half_share_grads(): pl.pallas_call(lambda *refs: half_share_kernel(*refs, plan=plan, low=low)...  7.18 us
    convert_element_type x14, other arithmetic, summed(): return total.astype(BF16)  6.65 us
    pallas_call x3, Pallas kernels, assemble(): pl.pallas_call(lambda *refs: assemble_kernel(*refs, plan=plan), in_specs=...  6.31 us
  transfers between devices with their start and end apart: 34, of which 18 were waited for; matrix products, arithmetic and copies ran while one was open for 17% of the time, Pallas kernels for 8%

profile of v2, /device:TPU:0, one launch (start us, length us, event | category | flops | bytes accessed | tf_op | source)
XLA Modules:
  0.0 238.0 jit_solution(3594414418377570467)
XLA Ops:
  0.7 3.0 %collective-permute-start.1 = (bf16[256,768]{1,0:T(8,128)(2,1)}, bf16[256,768]{1,0:T(8,128)(2,1)S(1)}, u32[]{:S(2)}, u32[]{:S(2)}) collective-permute-start(bf16[256,768]{1,0:T(8,128)(2,1)} %bitcast.146), channel_id=1, source_target_pairs={{0,2},{1,3},{2,0},{3,1},{4,6},{5,7},{6,4},{7,5},{8,10},{9,11},{10,... | collective-permute-start | bytes 1179656 | tf_op jit(solution)/shard_map/ppermute | solution.py:316
  5.4 8.5 %collective-permute-done.1 = bf16[256,768]{1,0:T(8,128)(2,1)S(1)} collective-permute-done((bf16[256,768]{1,0:T(8,128)(2,1)}, bf16[256,768]{1,0:T(8,128)(2,1)S(1)}, u32[]{:S(2)}, u32[]{:S(2)}) %collective-permute-start.1) | collective-permute-done | bytes 393248 | tf_op jit(solution)/shard_map/ppermute | solution.py:316
  13.9 1.3 convert_element_type.654
  15.2 1.3 convert_element_type.652
  16.5 1.3 convert_element_type.648
  19.3 1.3 convert_element_type.650
  20.6 1.3 convert_element_type.649
  21.9 1.3 convert_element_type.655
  23.1 1.3 convert_element_type.656
  24.5 1.9 fusion.27.q_ref
  26.4 2.6 %convolution_convert_fusion.2.k_ref = bf16[1024,768]{1,0:T(8,128)(2,1)S(1)} fusion(bf16[768,768]{1,0:T(8,128)(2,1)S(1)} %copy-done, bf16[256,768]{1,0:T(8,128)(2,1)S(1)} %collective-permute-done.2, bf16[256,768]{1,0:T(8,128)(2,1)S(1)} %collective-permute-done.1, bf16[256,768]{1,0:T(8,128)(2,1)S(1)} %collective-permute-done, bf16[256,768]{1,0:T(8,128)(2,1)} %bitcast.148), kind=kOutput, calls=%fused_computation.39 | convolution fusion | flops 1215037440 | bytes 4325376 | tf_op jit(solution)/shard_map/dot_general | solution.py:32
  29.1 1.4 add_convert_fusion.1.v_ref
  30.5 9.5 %attn_fwd.1 = (bf16[256,768]{1,0:T(8,128)(2,1)S(1)}, f32[256,768]{1,0:T(8,128)S(1)}) custom-call(bf16[256,768]{1,0:T(8,128)(2,1)S(1)} %fusion.27.q_ref, bf16[1024,768]{1,0:T(8,128)(2,1)S(1)} %convolution_convert_fusion.2.k_ref, bf16[1024,768]{1,0:T(8,128)(2,1)S(1)} %add_convert_fusion.1.v_ref, f32[4,1024]{1,0:T(4,128)S(1)} %reshape.946.bias_ref), custom_call_target="tpu_custom_call" | custom-call | tf_op jit(solution)/shard_map/attn_fwd/pallas_call | solution.py:127
  40.0 2.1 collective-permute-start.13
  43.1 8.8 %collective-permute-done.13.refs_7_ = bf16[256,768]{1,0:T(8,128)(2,1)S(1)} collective-permute-done((bf16[256,768]{1,0:T(8,128)(2,1)S(1)}, bf16[256,768]{1,0:T(8,128)(2,1)S(1)}, u32[]{:S(2)}, u32[]{:S(2)}) %collective-permute-start.13) | collective-permute-done | bytes 393248 | tf_op jit(solution)/shard_map/ppermute | solution.py:316
  53.1 3.9 %multiply_convert_fusion = (bf16[256,3072]{1,0:T(8,128)(2,1)S(1)}, f32[256,3072]{1,0:T(8,128)}) fusion(f32[3072]{0:T(1024)S(1)} %copy-done.22, bf16[256,768]{1,0:T(8,128)(2,1)S(1)} %get-tuple-element.84.refs_3_, bf16[768,3072]{1,0:T(8,128)(2,1)S(1)} %bitcast.159), kind=kOutput, calls=%fused_computation.34 | convolution fusion | flops 1215823872 | bytes 9842688 | tf_op jit(solution)/shard_map/dot_general | solution.py:32
  57.0 1.6 fusion.79
  58.6 2.2 multiply_convert_fusion.1
  60.9 1.6 fusion.80
  63.3 1.4 fusion.73
  65.3 3.1 %fusion.7.refs_4_ = bf16[256,3072]{1,0:T(8,128)(2,1)S(1)} fusion(f32[256,3072]{1,0:T(8,128)S(1)} %copy-done.26, bf16[256,768]{1,0:T(8,128)(2,1)S(1)} %add_convert_fusion.8.refs_4_, bf16[3072,768]{1,0:T(8,128)(2,1)S(1)} %bitcast.157), kind=kOutput, calls=%fused_computation.19 | convolution fusion | flops 1225261056 | bytes 9830400 | tf_op jit(solution)/shard_map/dot_general | solution.py:32
  68.5 1.6 multiply_reduce_fusion.1
  70.3 3.1 %convert_reduce_fusion = (f32[3072]{0:T(1024)S(1)}, bf16[256,3072]{1,0:T(8,128)(2,1)S(1)}) fusion(f32[256,3072]{1,0:T(8,128)S(1)} %get-tuple-element.101, bf16[256,768]{1,0:T(8,128)(2,1)S(1)} %get-tuple-element.58.refs_2_, bf16[3072,768]{1,0:T(8,128)(2,1)S(1)} %bitcast.157), kind=kOutput, calls=%fused_computation.32 | convolution fusion | flops 1226830848 | bytes 9842688 | tf_op jit(solution)/shard_map/dot_general | solution.py:32
  73.4 1.7 multiply_reduce_fusion
  75.2 1.3 fusion.72
  77.2 3.1 %grads_down.1 = (bf16[1,2,4,192,384]{4,3,2,1,0:T(8,128)(2,1)S(1)}, bf16[1,2,4,192,384]{4,3,2,1,0:T(8,128)(2,1)S(1)}) custom-call(s32[4]{0:T(128)S(1)} %pad_add_fusion.refs_0_, bf16[256,3072]{1,0:T(8,128)(2,1)S(1)} %get-tuple-element.100.refs_1_, bf16[256,768]{1,0:T(8,128)(2,1)S(1)} %get-tuple-element.58.refs_2_, bf16[256,3072]{1,0:T(8,128)(2,1)} %copy-done.9, ...), custom_call_target="tpu_custom_call" | custom-call | tf_op jit(solution)/shard_map/grads_down/pallas_call | solution.py:226
  80.3 14.5 %attn_bwd.1 = (bf16[256,768]{1,0:T(8,128)(2,1)S(1)}, bf16[1024,768]{1,0:T(8,128)(2,1)S(1)}, bf16[1024,768]{1,0:T(8,128)(2,1)}) custom-call(bf16[256,768]{1,0:T(8,128)(2,1)S(1)} %fusion.27.q_ref, bf16[1024,768]{1,0:T(8,128)(2,1)} %copy-done.1, bf16[1024,768]{1,0:T(8,128)(2,1)} %copy-done.2, f32[4,1024]{1,0:T(4,128)S(1)} %reshape.946.bias_ref, ...), custom_call_target="tpu_custom_call" | custom-call | tf_op jit(solution)/shard_map/attn_bwd/pallas_call | solution.py:143
  95.0 1.8 convert_reduce_fusion.1
  96.7 1.4 copy-done.3
  98.1 5.5 %grads_qkv.1 = (bf16[2,2,4,144,384]{4,3,2,1,0:T(8,128)(2,1)}, bf16[2,2,4,144,384]{4,3,2,1,0:T(8,128)(2,1)}) custom-call(s32[4]{0:T(128)S(1)} %pad_add_fusion.refs_0_, bf16[1024,768]{1,0:T(8,128)(2,1)S(1)} %pad_maximum_fusion.refs_1_, bf16[256,768]{1,0:T(8,128)(2,1)S(1)} %get-tuple-element.35.refs_2_, bf16[1024,768]{1,0:T(8,128)(2,1)S(1)} %get-tuple-element.36.refs_3_, ...), custom_call_target="tpu_custom_call" | custom-call | tf_op jit(solution)/shard_map/grads_qkv/pallas_call | solution.py:268
  103.8 4.1 %grads_up_proj.1 = (bf16[1,2,4,240,384]{4,3,2,1,0:T(8,128)(2,1)S(1)}, bf16[1,2,4,240,384]{4,3,2,1,0:T(8,128)(2,1)S(1)}) custom-call(s32[4]{0:T(128)S(1)} %pad_add_fusion.refs_0_, bf16[256,768]{1,0:T(8,128)(2,1)S(1)} %get-tuple-element.85.refs_1_, bf16[256,3072]{1,0:T(8,128)(2,1)} %copy-done.11, bf16[256,768]{1,0:T(8,128)(2,1)S(1)} %get-tuple-element.84.refs_3_, ...), custom_call_target="tpu_custom_call" | custom-call | tf_op jit(solution)/shard_map/grads_up_proj/pallas_call | solution.py:226
  109.1 4.0 %collective-permute-done.29 = f32[9216]{0:T(1024)S(1)} collective-permute-done((f32[9216]{0:T(1024)S(1)}, f32[9216]{0:T(1024)S(1)}, u32[]{:S(2)}, u32[]{:S(2)}) %collective-permute-start.29) | collective-permute-done | bytes 36896 | tf_op jit(solution)/shard_map/ppermute | solution.py:316
  113.0 1.9 collective-permute-start.30
  114.9 1.4 fusion.81
  117.1 1.7 collective-permute-start.31
  119.4 1.4 add_convert_fusion
  121.5 1.8 collective-permute-start.32
  123.4 1.6 collective-permute-start.16
  125.0 1.4 add_convert_fusion.2
  126.4 1.6 collective-permute-start.6
  128.0 7.3 %collective-permute-done.23 = bf16[1,4,192,384]{3,2,1,0:T(8,128)(2,1)S(1)} collective-permute-done((bf16[1,4,192,384]{3,2,1,0:T(8,128)(2,1)S(1)}, bf16[1,4,192,384]{3,2,1,0:T(8,128)(2,1)S(1)}, u32[]{:S(2)}, u32[]{:S(2)}) %collective-permute-start.23) | collective-permute-done | bytes 589856 | tf_op jit(solution)/shard_map/ppermute | solution.py:316
  135.4 1.6 collective-permute-start.24
  137.6 2.7 %collective-permute-start.33 = (f32[9216]{0:T(1024)S(1)}, f32[9216]{0:T(1024)S(1)}, u32[]{:S(2)}, u32[]{:S(2)}) collective-permute-start(f32[9216]{0:T(1024)S(1)} %add.761), channel_id=1, source_target_pairs={{0,16},{4,20},{8,24},{12,28},{16,0},{20,4},{24,8},{28,12},{1,17},{... | collective-permute-start | bytes 110600 | tf_op jit(solution)/shard_map/ppermute | solution.py:316
  140.3 1.9 collective-permute-done.24
  142.3 3.7 %collective-permute-start.25 = (bf16[1,192,384]{2,1,0:T(8,128)(2,1)S(1)}, bf16[1,192,384]{2,1,0:T(8,128)(2,1)S(1)}, u32[]{:S(2)}, u32[]{:S(2)}) collective-permute-start(bf16[1,192,384]{2,1,0:T(8,128)(2,1)S(1)} %fusion.49), channel_id=1, source_target_pairs={{0,16},{4,20},{8,24},{12,28},{16,0},{20,4},{24,8},{28,12},{1,17},{... | collective-permute-start | bytes 442376 | tf_op jit(solution)/shard_map/ppermute | solution.py:316
  146.0 3.4 %collective-permute-done.16 = bf16[1,4,240,384]{3,2,1,0:T(8,128)(2,1)S(1)} collective-permute-done((bf16[1,4,240,384]{3,2,1,0:T(8,128)(2,1)S(1)}, bf16[1,4,240,384]{3,2,1,0:T(8,128)(2,1)S(1)}, u32[]{:S(2)}, u32[]{:S(2)}) %collective-permute-start.16) | collective-permute-done | bytes 737312 | tf_op jit(solution)/shard_map/ppermute | solution.py:316
  149.5 1.7 collective-permute-start.17
  151.3 2.7 %collective-permute-start.26 = (bf16[1,192,384]{2,1,0:T(8,128)(2,1)S(1)}, bf16[1,192,384]{2,1,0:T(8,128)(2,1)S(1)}, u32[]{:S(2)}, u32[]{:S(2)}) collective-permute-start(bf16[1,192,384]{2,1,0:T(8,128)(2,1)S(1)} %fusion.52.refs_1_), channel_id=1, source_target_pairs={{0,16},{4,20},{8,24},{12,28},{16,0},{20,4},{24,8},{28,12},{1,17},{... | collective-permute-start | bytes 442376 | tf_op jit(solution)/shard_map/ppermute | solution.py:316
  156.5 4.3 %collective-permute-done.26.refs_2_ = bf16[1,192,384]{2,1,0:T(8,128)(2,1)S(1)} collective-permute-done((bf16[1,192,384]{2,1,0:T(8,128)(2,1)S(1)}, bf16[1,192,384]{2,1,0:T(8,128)(2,1)S(1)}, u32[]{:S(2)}, u32[]{:S(2)}) %collective-permute-start.26) | collective-permute-done | bytes 147488 | tf_op jit(solution)/shard_map/ppermute | solution.py:316
  160.8 3.7 %collective-permute-start.27 = (bf16[2,192,384]{2,1,0:T(8,128)(2,1)S(1)}, bf16[2,192,384]{2,1,0:T(8,128)(2,1)S(1)}, u32[]{:S(2)}, u32[]{:S(2)}) collective-permute-start(bf16[2,192,384]{2,1,0:T(8,128)(2,1)S(1)} %pad_maximum_fusion.5), channel_id=1, source_target_pairs={{0,8},{4,12},{8,0},{12,4},{16,24},{20,28},{24,16},{28,20},{1,9},{5... | collective-permute-start | bytes 884744 | tf_op jit(solution)/shard_map/ppermute | solution.py:316
  166.2 2.4 collective-permute-start.8
  168.6 7.4 %collective-permute-done.18 = bf16[1,240,384]{2,1,0:T(8,128)(2,1)S(1)} collective-permute-done((bf16[1,240,384]{2,1,0:T(8,128)(2,1)S(1)}, bf16[1,240,384]{2,1,0:T(8,128)(2,1)S(1)}, u32[]{:S(2)}, u32[]{:S(2)}) %collective-permute-start.18) | collective-permute-done | bytes 184352 | tf_op jit(solution)/shard_map/ppermute | solution.py:316
  176.1 3.4 %collective-permute-start.19 = (bf16[1,240,384]{2,1,0:T(8,128)(2,1)S(1)}, bf16[1,240,384]{2,1,0:T(8,128)(2,1)S(1)}, u32[]{:S(2)}, u32[]{:S(2)}) collective-permute-start(bf16[1,240,384]{2,1,0:T(8,128)(2,1)S(1)} %fusion.47.refs_1_), channel_id=1, source_target_pairs={{0,16},{4,20},{8,24},{12,28},{16,0},{20,4},{24,8},{28,12},{1,17},{... | collective-permute-start | bytes 552968 | tf_op jit(solution)/shard_map/ppermute | solution.py:316
  180.5 1.8 collective-permute-start.9
  182.3 6.2 %collective-permute-done.19.refs_2_ = bf16[1,240,384]{2,1,0:T(8,128)(2,1)S(1)} collective-permute-done((bf16[1,240,384]{2,1,0:T(8,128)(2,1)S(1)}, bf16[1,240,384]{2,1,0:T(8,128)(2,1)S(1)}, u32[]{:S(2)}, u32[]{:S(2)}) %collective-permute-start.19) | collective-permute-done | bytes 184352 | tf_op jit(solution)/shard_map/ppermute | solution.py:316
  190.9 1.6 collective-permute-start.4
  192.5 5.2 %collective-permute-done.10.refs_2_ = bf16[1,144,384]{2,1,0:T(8,128)(2,1)S(1)} collective-permute-done((bf16[1,144,384]{2,1,0:T(8,128)(2,1)S(1)}, bf16[1,144,384]{2,1,0:T(8,128)(2,1)S(1)}, u32[]{:S(2)}, u32[]{:S(2)}) %collective-permute-start.10) | collective-permute-done | bytes 110624 | tf_op jit(solution)/shard_map/ppermute | solution.py:316
  198.2 1.7 collective-permute-done.20.refs_3_
  200.7 1.6 collective-permute-start.28
  202.3 1.5 collective-permute-done.11.refs_3_
  206.0 25.0 %collective-permute-done.28.refs_4_ = bf16[4,192,384]{2,1,0:T(8,128)(2,1)S(1)} collective-permute-done((bf16[4,192,384]{2,1,0:T(8,128)(2,1)S(1)}, bf16[4,192,384]{2,1,0:T(8,128)(2,1)S(1)}, u32[]{:S(2)}, u32[]{:S(2)}) %collective-permute-start.28) | collective-permute-done | bytes 589856 | tf_op jit(solution)/shard_map/ppermute | solution.py:316
  231.0 2.1 assemble_down.1
  233.1 2.3 assemble_up.1
  235.7 1.9 assemble_qkv.1
  (180 shorter events, 23.0 us)
Async XLA Ops:
  0.7 25.8 %copy-start = (bf16[768,768]{1,0:T(8,128)(2,1)S(1)}, bf16[768,768]{1,0:T(8,128)(2,1)}, u32[]{:S(2)}) copy-start(bf16[768,768]{1,0:T(8,128)(2,1)} %param.22) | copy-start | bytes 3538948
  0.7 13.2 %collective-permute-start.1 = (bf16[256,768]{1,0:T(8,128)(2,1)}, bf16[256,768]{1,0:T(8,128)(2,1)S(1)}, u32[]{:S(2)}, u32[]{:S(2)}) collective-permute-start(bf16[256,768]{1,0:T(8,128)(2,1)} %bitcast.146), channel_id=1, source_target_pairs={{0,2},{1,3},{2,0},{3,1},{4,6},{5,7},{6,4},{7,5},{8,10},{9,11},{10,... | collective-permute-start | bytes 1179656 | tf_op jit(solution)/shard_map/ppermute | solution.py:316
  3.7 22.7 %collective-permute-start = (bf16[256,768]{1,0:T(8,128)(2,1)}, bf16[256,768]{1,0:T(8,128)(2,1)S(1)}, u32[]{:S(2)}, u32[]{:S(2)}) collective-permute-start(bf16[256,768]{1,0:T(8,128)(2,1)} %bitcast.147), channel_id=1, source_target_pairs={{0,1},{1,0},{2,3},{3,2},{4,5},{5,4},{6,7},{7,6},{8,9},{9,8},{10,11... | collective-permute-start | bytes 1179656 | tf_op jit(solution)/shard_map/ppermute | solution.py:316
  3.7 59.0 %collective-permute-start.14 = (bf16[256,768]{1,0:T(8,128)(2,1)}, bf16[256,768]{1,0:T(8,128)(2,1)S(1)}, u32[]{:S(2)}, u32[]{:S(2)}) collective-permute-start(bf16[256,768]{1,0:T(8,128)(2,1)} %bitcast.154), channel_id=1, source_target_pairs={{0,2},{1,3},{2,0},{3,1},{4,6},{5,7},{6,4},{7,5},{8,10},{9,11},{10,... | collective-permute-start | bytes 1179656 | tf_op jit(solution)/shard_map/ppermute | solution.py:316
  13.9 12.6 %collective-permute-start.2 = (bf16[256,768]{1,0:T(8,128)(2,1)S(1)}, bf16[256,768]{1,0:T(8,128)(2,1)S(1)}, u32[]{:S(2)}, u32[]{:S(2)}) collective-permute-start(bf16[256,768]{1,0:T(8,128)(2,1)S(1)} %collective-permute-done.1), channel_id=1, source_target_pairs={{0,1},{1,0},{2,3},{3,2},{4,5},{5,4},{6,7},{7,6},{8,9},{9,8},{10,11... | collective-permute-start | bytes 1179656 | tf_op jit(solution)/shard_map/ppermute | solution.py:316
  26.4 2.6 %copy-start.8 = (bf16[1,256,768]{2,1,0:T(8,128)(2,1)S(1)}, bf16[1,256,768]{2,1,0:T(8,128)(2,1)}, u32[]{:S(2)}) copy-start(bf16[1,256,768]{2,1,0:T(8,128)(2,1)} %param.19) | copy-start | bytes 1179652
  26.4 2.6 %copy-start.24 = (bf16[768,768]{1,0:T(8,128)(2,1)S(1)}, bf16[768,768]{1,0:T(8,128)(2,1)}, u32[]{:S(2)}) copy-start(bf16[768,768]{1,0:T(8,128)(2,1)} %param.23) | copy-start | bytes 3538948
  26.4 2.6 %copy-start.14 = (bf16[256,768]{1,0:T(8,128)(2,1)}, bf16[256,768]{1,0:T(8,128)(2,1)S(1)}, u32[]{:S(2)}) copy-start(bf16[256,768]{1,0:T(8,128)(2,1)S(1)} %collective-permute-done.2) | copy-start | bytes 1179652
  29.0 1.4 copy-start.1
  30.5 12.2 %copy-start.2 = (bf16[1024,768]{1,0:T(8,128)(2,1)}, bf16[1024,768]{1,0:T(8,128)(2,1)S(1)}, u32[]{:S(2)}) copy-start(bf16[1024,768]{1,0:T(8,128)(2,1)S(1)} %add_convert_fusion.1.v_ref) | copy-start | bytes 4718596
  30.5 11.6 %copy-start.5 = (bf16[768,768]{1,0:T(8,128)(2,1)S(1)}, bf16[768,768]{1,0:T(8,128)(2,1)}, u32[]{:S(2)}) copy-start(bf16[768,768]{1,0:T(8,128)(2,1)} %param.25) | copy-start | bytes 3538948
  30.5 11.6 %copy-start.16 = (f32[768]{0:T(1024)S(1)}, f32[768]{0:T(1024)}, u32[]{:S(2)}) copy-start(f32[768]{0:T(1024)} %convert_element_type.648) | copy-start | bytes 9220
  30.5 12.4 %copy-start.15 = (bf16[256,768]{1,0:T(8,128)(2,1)S(1)}, bf16[256,768]{1,0:T(8,128)(2,1)}, u32[]{:S(2)}) copy-start(bf16[256,768]{1,0:T(8,128)(2,1)} %copy-done.14) | copy-start | bytes 1179652
  40.0 11.9 %collective-permute-start.13 = (bf16[256,768]{1,0:T(8,128)(2,1)S(1)}, bf16[256,768]{1,0:T(8,128)(2,1)S(1)}, u32[]{:S(2)}, u32[]{:S(2)}) collective-permute-start(bf16[256,768]{1,0:T(8,128)(2,1)S(1)} %get-tuple-element.33.refs_5_), channel_id=1, source_target_pairs={{0,2},{1,3},{2,0},{3,1},{4,6},{5,7},{6,4},{7,5},{8,10},{9,11},{10,... | collective-permute-start | bytes 1179656 | tf_op jit(solution)/shard_map/ppermute | solution.py:316
  42.1 11.0 %slice-start.2 = ((s8[4718592]{0:T(1024)(128)(4,1)}), s8[4194304]{0:T(1024)(128)(4,1)S(1)}, s32[]{:S(2)}) async-start(s8[4718592]{0:T(1024)(128)(4,1)} %bitcast.158), calls=%async_computation.2 | async-start | bytes 8388608
  42.9 9.8 %copy-start.18 = (f32[768]{0:T(1024)S(1)}, f32[768]{0:T(1024)}, u32[]{:S(2)}) copy-start(f32[768]{0:T(1024)} %convert_element_type.649) | copy-start | bytes 9220
  42.9 9.8 %copy-start.20 = (f32[768]{0:T(1024)S(1)}, f32[768]{0:T(1024)}, u32[]{:S(2)}) copy-start(f32[768]{0:T(1024)} %convert_element_type.650) | copy-start | bytes 9220
  42.9 10.1 %slice-start.3 = ((s8[4718592]{0:T(1024)(128)(4,1)}), s8[524288]{0:T(1024)(128)(4,1)S(1)}, s32[]{:S(2)}) async-start(s8[4718592]{0:T(1024)(128)(4,1)} %bitcast.158), calls=%async_computation.3 | async-start | bytes 1048576
  43.1 10.0 %copy-start.22 = (f32[3072]{0:T(1024)S(1)}, f32[3072]{0:T(1024)}, u32[]{:S(2)}) copy-start(f32[3072]{0:T(1024)} %convert_element_type.652) | copy-start | bytes 36868
  52.7 4.3 %slice-start = ((s8[4718592]{0:T(1024)(128)(4,1)}), s8[4194304]{0:T(1024)(128)(4,1)S(1)}, s32[]{:S(2)}) async-start(s8[4718592]{0:T(1024)(128)(4,1)} %bitcast.156), calls=%async_computation | async-start | bytes 8388608
  53.1 3.9 %copy-start.23 = (f32[768]{0:T(1024)S(1)}, f32[768]{0:T(1024)}, u32[]{:S(2)}) copy-start(f32[768]{0:T(1024)} %convert_element_type.654) | copy-start | bytes 9220
  53.1 3.9 %slice-start.1 = ((s8[4718592]{0:T(1024)(128)(4,1)}), s8[524288]{0:T(1024)(128)(4,1)S(1)}, s32[]{:S(2)}) async-start(s8[4718592]{0:T(1024)(128)(4,1)} %bitcast.156), calls=%async_computation.1 | async-start | bytes 1048576
  57.0 1.6 copy-start.9
  60.8 1.9 copy-start.12
  60.8 1.9 copy-start.19
  63.3 2.0 copy-start.26
  68.5 1.6 copy-start.10
  73.4 1.7 copy-start.11
  95.0 8.7 %copy-start.6 = (f32[256,768]{1,0:T(8,128)S(1)}, f32[256,768]{1,0:T(8,128)}, u32[]{:S(2)}) copy-start(f32[256,768]{1,0:T(8,128)} %get-tuple-element.62) | copy-start | bytes 2359300
  96.7 1.4 copy-start.3
  103.6 21.4 %collective-permute-start.5 = (bf16[2,2,4,144,384]{4,3,2,1,0:T(8,128)(2,1)}, bf16[2,2,4,144,384]{4,3,2,1,0:T(8,128)(2,1)}, u32[]{:S(2)}, u32[]{:S(2)}) collective-permute-start(bf16[2,2,4,144,384]{4,3,2,1,0:T(8,128)(2,1)} %get-tuple-element.39), channel_id=1, source_target_pairs={{0,1},{1,0},{2,3},{3,2},{4,5},{5,4},{6,7},{7,6},{8,9},{9,8},{10,11... | collective-permute-start | bytes 5308424 | tf_op jit(solution)/shard_map/ppermute | solution.py:316
  103.6 4.8 %copy-start.17 = (f32[9216]{0:T(1024)S(1)}, f32[9216]{0:T(1024)}, u32[]{:S(2)}) copy-start(f32[9216]{0:T(1024)} %custom-call) | copy-start | bytes 110596
  107.8 15.4 %collective-permute-start.15 = (bf16[1,2,4,240,384]{4,3,2,1,0:T(8,128)(2,1)S(1)}, bf16[1,2,4,240,384]{4,3,2,1,0:T(8,128)(2,1)S(1)}, u32[]{:S(2)}, u32[]{:S(2)}) collective-permute-start(bf16[1,2,4,240,384]{4,3,2,1,0:T(8,128)(2,1)S(1)} %get-tuple-element.44), channel_id=1, source_target_pairs={{0,1},{1,0},{2,3},{3,2},{4,5},{5,4},{6,7},{7,6},{8,9},{9,8},{10,11... | collective-permute-start | bytes 4423688 | tf_op jit(solution)/shard_map/ppermute | solution.py:316
  108.4 10.4 %collective-permute-start.22 = (bf16[1,2,4,192,384]{4,3,2,1,0:T(8,128)(2,1)S(1)}, bf16[1,2,4,192,384]{4,3,2,1,0:T(8,128)(2,1)S(1)}, u32[]{:S(2)}, u32[]{:S(2)}) collective-permute-start(bf16[1,2,4,192,384]{4,3,2,1,0:T(8,128)(2,1)S(1)} %get-tuple-element.48), channel_id=1, source_target_pairs={{0,1},{1,0},{2,3},{3,2},{4,5},{5,4},{6,7},{7,6},{8,9},{9,8},{10,11... | collective-permute-start | bytes 3538952 | tf_op jit(solution)/shard_map/ppermute | solution.py:316
  108.6 4.4 %collective-permute-start.29 = (f32[9216]{0:T(1024)S(1)}, f32[9216]{0:T(1024)S(1)}, u32[]{:S(2)}, u32[]{:S(2)}) collective-permute-start(f32[9216]{0:T(1024)S(1)} %constant_dynamic-update-slice_fusion), channel_id=1, source_target_pairs={{0,1},{1,0},{2,3},{3,2},{4,5},{5,4},{6,7},{7,6},{8,9},{9,8},{10,11... | collective-permute-start | bytes 110600 | tf_op jit(solution)/shard_map/ppermute | solution.py:316
  113.0 6.3 %copy-start.4 = (bf16[1024,768]{1,0:T(8,128)(2,1)S(1)}, bf16[1024,768]{1,0:T(8,128)(2,1)}, u32[]{:S(2)}) copy-start(bf16[1024,768]{1,0:T(8,128)(2,1)} %get-tuple-element.37.refs_4_) | copy-start | bytes 4718596
  113.0 6.3 %copy-start.25 = (bf16[768,768]{1,0:T(8,128)(2,1)S(1)}, bf16[768,768]{1,0:T(8,128)(2,1)}, u32[]{:S(2)}) copy-start(bf16[768,768]{1,0:T(8,128)(2,1)} %param.23) | copy-start | bytes 3538948
  113.0 4.0 %collective-permute-start.30 = (f32[9216]{0:T(1024)S(1)}, f32[9216]{0:T(1024)S(1)}, u32[]{:S(2)}, u32[]{:S(2)}) collective-permute-start(f32[9216]{0:T(1024)S(1)} %add.758), channel_id=1, source_target_pairs={{0,2},{1,3},{2,0},{3,1},{4,6},{5,7},{6,4},{7,5},{8,10},{9,11},{10,... | collective-permute-start | bytes 110600 | tf_op jit(solution)/shard_map/ppermute | solution.py:316
  117.1 4.4 %collective-permute-start.31 = (f32[9216]{0:T(1024)S(1)}, f32[9216]{0:T(1024)S(1)}, u32[]{:S(2)}, u32[]{:S(2)}) collective-permute-start(f32[9216]{0:T(1024)S(1)} %add.759), channel_id=1, source_target_pairs={{0,4},{4,0},{8,12},{12,8},{16,20},{20,16},{24,28},{28,24},{1,5},{5... | collective-permute-start | bytes 110600 | tf_op jit(solution)/shard_map/ppermute | solution.py:316
  118.9 6.1 %copy-start.7 = (bf16[2,2,4,144,384]{4,3,2,1,0:T(8,128)(2,1)S(1)}, bf16[2,2,4,144,384]{4,3,2,1,0:T(8,128)(2,1)}, u32[]{:S(2)}) copy-start(bf16[2,2,4,144,384]{4,3,2,1,0:T(8,128)(2,1)} %get-tuple-element.38) | copy-start | bytes 5308420
  119.0 16.3 %collective-permute-start.23 = (bf16[1,4,192,384]{3,2,1,0:T(8,128)(2,1)S(1)}, bf16[1,4,192,384]{3,2,1,0:T(8,128)(2,1)S(1)}, u32[]{:S(2)}, u32[]{:S(2)}) collective-permute-start(bf16[1,4,192,384]{3,2,1,0:T(8,128)(2,1)S(1)} %fusion.38), channel_id=1, source_target_pairs={{0,4},{4,0},{8,12},{12,8},{16,20},{20,16},{24,28},{28,24},{1,5},{5... | collective-permute-start | bytes 1769480 | tf_op jit(solution)/shard_map/ppermute | solution.py:316
  120.8 16.3 %copy-start.13 = (bf16[768,768]{1,0:T(8,128)(2,1)S(1)}, bf16[768,768]{1,0:T(8,128)(2,1)}, u32[]{:S(2)}) copy-start(bf16[768,768]{1,0:T(8,128)(2,1)} %param.20) | copy-start | bytes 3538948
  121.5 16.1 %collective-permute-start.32 = (f32[9216]{0:T(1024)S(1)}, f32[9216]{0:T(1024)S(1)}, u32[]{:S(2)}, u32[]{:S(2)}) collective-permute-start(f32[9216]{0:T(1024)S(1)} %add.760), channel_id=1, source_target_pairs={{0,8},{4,12},{8,0},{12,4},{16,24},{20,28},{24,16},{28,20},{1,9},{5... | collective-permute-start | bytes 110600 | tf_op jit(solution)/shard_map/ppermute | solution.py:316
  123.4 26.0 %collective-permute-start.16 = (bf16[1,4,240,384]{3,2,1,0:T(8,128)(2,1)S(1)}, bf16[1,4,240,384]{3,2,1,0:T(8,128)(2,1)S(1)}, u32[]{:S(2)}, u32[]{:S(2)}) collective-permute-start(bf16[1,4,240,384]{3,2,1,0:T(8,128)(2,1)S(1)} %fusion.34), channel_id=1, source_target_pairs={{0,4},{4,0},{8,12},{12,8},{16,20},{20,16},{24,28},{28,24},{1,5},{5... | collective-permute-start | bytes 2211848 | tf_op jit(solution)/shard_map/ppermute | solution.py:316
  126.4 27.5 %collective-permute-start.6 = (bf16[1,2,4,144,384]{4,3,2,1,0:T(8,128)(2,1)S(1)}, bf16[1,2,4,144,384]{4,3,2,1,0:T(8,128)(2,1)S(1)}, u32[]{:S(2)}, u32[]{:S(2)}) collective-permute-start(bf16[1,2,4,144,384]{4,3,2,1,0:T(8,128)(2,1)S(1)} %add_convert_fusion.2), channel_id=1, source_target_pairs={{0,2},{1,3},{2,0},{3,1},{4,6},{5,7},{6,4},{7,5},{8,10},{9,11},{10,... | collective-permute-start | bytes 2654216 | tf_op jit(solution)/shard_map/ppermute | solution.py:316
  135.4 6.8 %collective-permute-start.24 = (bf16[2,192,384]{2,1,0:T(8,128)(2,1)S(1)}, bf16[2,192,384]{2,1,0:T(8,128)(2,1)S(1)}, u32[]{:S(2)}, u32[]{:S(2)}) collective-permute-start(bf16[2,192,384]{2,1,0:T(8,128)(2,1)S(1)} %fusion.39), channel_id=1, source_target_pairs={{0,8},{4,12},{8,0},{12,4},{16,24},{20,28},{24,16},{28,20},{1,9},{5... | collective-permute-start | bytes 884744 | tf_op jit(solution)/shard_map/ppermute | solution.py:316
  137.6 18.2 %collective-permute-start.33 = (f32[9216]{0:T(1024)S(1)}, f32[9216]{0:T(1024)S(1)}, u32[]{:S(2)}, u32[]{:S(2)}) collective-permute-start(f32[9216]{0:T(1024)S(1)} %add.761), channel_id=1, source_target_pairs={{0,16},{4,20},{8,24},{12,28},{16,0},{20,4},{24,8},{28,12},{1,17},{... | collective-permute-start | bytes 110600 | tf_op jit(solution)/shard_map/ppermute | solution.py:316
  142.3 8.9 %collective-permute-start.25 = (bf16[1,192,384]{2,1,0:T(8,128)(2,1)S(1)}, bf16[1,192,384]{2,1,0:T(8,128)(2,1)S(1)}, u32[]{:S(2)}, u32[]{:S(2)}) collective-permute-start(bf16[1,192,384]{2,1,0:T(8,128)(2,1)S(1)} %fusion.49), channel_id=1, source_target_pairs={{0,16},{4,20},{8,24},{12,28},{16,0},{20,4},{24,8},{28,12},{1,17},{... | collective-permute-start | bytes 442376 | tf_op jit(solution)/shard_map/ppermute | solution.py:316
  149.5 15.0 %collective-permute-start.17 = (bf16[2,240,384]{2,1,0:T(8,128)(2,1)S(1)}, bf16[2,240,384]{2,1,0:T(8,128)(2,1)S(1)}, u32[]{:S(2)}, u32[]{:S(2)}) collective-permute-start(bf16[2,240,384]{2,1,0:T(8,128)(2,1)S(1)} %fusion.35), channel_id=1, source_target_pairs={{0,8},{4,12},{8,0},{12,4},{16,24},{20,28},{24,16},{28,20},{1,9},{5... | collective-permute-start | bytes 1105928 | tf_op jit(solution)/shard_map/ppermute | solution.py:316
  151.3 9.5 %collective-permute-start.26 = (bf16[1,192,384]{2,1,0:T(8,128)(2,1)S(1)}, bf16[1,192,384]{2,1,0:T(8,128)(2,1)S(1)}, u32[]{:S(2)}, u32[]{:S(2)}) collective-permute-start(bf16[1,192,384]{2,1,0:T(8,128)(2,1)S(1)} %fusion.52.refs_1_), channel_id=1, source_target_pairs={{0,16},{4,20},{8,24},{12,28},{16,0},{20,4},{24,8},{28,12},{1,17},{... | collective-permute-start | bytes 442376 | tf_op jit(solution)/shard_map/ppermute | solution.py:316
  155.1 10.0 %collective-permute-start.7 = (bf16[1,4,144,384]{3,2,1,0:T(8,128)(2,1)S(1)}, bf16[1,4,144,384]{3,2,1,0:T(8,128)(2,1)S(1)}, u32[]{:S(2)}, u32[]{:S(2)}) collective-permute-start(bf16[1,4,144,384]{3,2,1,0:T(8,128)(2,1)S(1)} %fusion.40), channel_id=1, source_target_pairs={{0,4},{4,0},{8,12},{12,8},{16,20},{20,16},{24,28},{28,24},{1,5},{5... | collective-permute-start | bytes 1327112 | tf_op jit(solution)/shard_map/ppermute | solution.py:316
  155.8 35.1 %collective-permute-start.3 = (bf16[2,256,768]{2,1,0:T(8,128)(2,1)S(1)}, bf16[2,256,768]{2,1,0:T(8,128)(2,1)S(1)}, u32[]{:S(2)}, u32[]{:S(2)}) collective-permute-start(bf16[2,256,768]{2,1,0:T(8,128)(2,1)S(1)} %slice_bitcast_fusion), channel_id=1, source_target_pairs={{0,1},{1,0},{2,3},{3,2},{4,5},{5,4},{6,7},{7,6},{8,9},{9,8},{10,11... | collective-permute-start | bytes 2359304 | tf_op jit(solution)/shard_map/ppermute | solution.py:316
  160.8 39.8 %collective-permute-start.27 = (bf16[2,192,384]{2,1,0:T(8,128)(2,1)S(1)}, bf16[2,192,384]{2,1,0:T(8,128)(2,1)S(1)}, u32[]{:S(2)}, u32[]{:S(2)}) collective-permute-start(bf16[2,192,384]{2,1,0:T(8,128)(2,1)S(1)} %pad_maximum_fusion.5), channel_id=1, source_target_pairs={{0,8},{4,12},{8,0},{12,4},{16,24},{20,28},{24,16},{28,20},{1,9},{5... | collective-permute-start | bytes 884744 | tf_op jit(solution)/shard_map/ppermute | solution.py:316
  164.6 11.3 %collective-permute-start.18 = (bf16[1,240,384]{2,1,0:T(8,128)(2,1)S(1)}, bf16[1,240,384]{2,1,0:T(8,128)(2,1)S(1)}, u32[]{:S(2)}, u32[]{:S(2)}) collective-permute-start(bf16[1,240,384]{2,1,0:T(8,128)(2,1)S(1)} %fusion.44), channel_id=1, source_target_pairs={{0,16},{4,20},{8,24},{12,28},{16,0},{20,4},{24,8},{28,12},{1,17},{... | collective-permute-start | bytes 552968 | tf_op jit(solution)/shard_map/ppermute | solution.py:316
  166.2 13.3 %collective-permute-start.8 = (bf16[2,144,384]{2,1,0:T(8,128)(2,1)S(1)}, bf16[2,144,384]{2,1,0:T(8,128)(2,1)S(1)}, u32[]{:S(2)}, u32[]{:S(2)}) collective-permute-start(bf16[2,144,384]{2,1,0:T(8,128)(2,1)S(1)} %fusion.41), channel_id=1, source_target_pairs={{0,8},{4,12},{8,0},{12,4},{16,24},{20,28},{24,16},{28,20},{1,9},{5... | collective-permute-start | bytes 663560 | tf_op jit(solution)/shard_map/ppermute | solution.py:316
  176.1 12.4 %collective-permute-start.19 = (bf16[1,240,384]{2,1,0:T(8,128)(2,1)S(1)}, bf16[1,240,384]{2,1,0:T(8,128)(2,1)S(1)}, u32[]{:S(2)}, u32[]{:S(2)}) collective-permute-start(bf16[1,240,384]{2,1,0:T(8,128)(2,1)S(1)} %fusion.47.refs_1_), channel_id=1, source_target_pairs={{0,16},{4,20},{8,24},{12,28},{16,0},{20,4},{24,8},{28,12},{1,17},{... | collective-permute-start | bytes 552968 | tf_op jit(solution)/shard_map/ppermute | solution.py:316
  180.5 9.3 %collective-permute-start.9 = (bf16[1,144,384]{2,1,0:T(8,128)(2,1)S(1)}, bf16[1,144,384]{2,1,0:T(8,128)(2,1)S(1)}, u32[]{:S(2)}, u32[]{:S(2)}) collective-permute-start(bf16[1,144,384]{2,1,0:T(8,128)(2,1)S(1)} %fusion.54), channel_id=1, source_target_pairs={{0,16},{4,20},{8,24},{12,28},{16,0},{20,4},{24,8},{28,12},{1,17},{... | collective-permute-start | bytes 331784 | tf_op jit(solution)/shard_map/ppermute | solution.py:316
  188.6 11.4 %collective-permute-start.20 = (bf16[2,240,384]{2,1,0:T(8,128)(2,1)S(1)}, bf16[2,240,384]{2,1,0:T(8,128)(2,1)S(1)}, u32[]{:S(2)}, u32[]{:S(2)}) collective-permute-start(bf16[2,240,384]{2,1,0:T(8,128)(2,1)S(1)} %pad_maximum_fusion.4), channel_id=1, source_target_pairs={{0,8},{4,12},{8,0},{12,4},{16,24},{20,28},{24,16},{28,20},{1,9},{5... | collective-permute-start | bytes 1105928 | tf_op jit(solution)/shard_map/ppermute | solution.py:316
  190.7 7.0 %collective-permute-start.10 = (bf16[1,144,384]{2,1,0:T(8,128)(2,1)S(1)}, bf16[1,144,384]{2,1,0:T(8,128)(2,1)S(1)}, u32[]{:S(2)}, u32[]{:S(2)}) collective-permute-start(bf16[1,144,384]{2,1,0:T(8,128)(2,1)S(1)} %fusion.57.refs_1_), channel_id=1, source_target_pairs={{0,16},{4,20},{8,24},{12,28},{16,0},{20,4},{24,8},{28,12},{1,17},{... | collective-permute-start | bytes 331784 | tf_op jit(solution)/shard_map/ppermute | solution.py:316
  190.9 14.1 %collective-permute-start.4 = (bf16[1,256,768]{2,1,0:T(8,128)(2,1)S(1)}, bf16[1,256,768]{2,1,0:T(8,128)(2,1)S(1)}, u32[]{:S(2)}, u32[]{:S(2)}) collective-permute-start(bf16[1,256,768]{2,1,0:T(8,128)(2,1)S(1)} %fusion.33), channel_id=1, source_target_pairs={{0,2},{1,3},{2,0},{3,1},{4,6},{5,7},{6,4},{7,5},{8,10},{9,11},{10,... | collective-permute-start | bytes 1179656 | tf_op jit(solution)/shard_map/ppermute | solution.py:316
  197.8 6.0 %collective-permute-start.11 = (bf16[2,144,384]{2,1,0:T(8,128)(2,1)S(1)}, bf16[2,144,384]{2,1,0:T(8,128)(2,1)S(1)}, u32[]{:S(2)}, u32[]{:S(2)}) collective-permute-start(bf16[2,144,384]{2,1,0:T(8,128)(2,1)S(1)} %pad_maximum_fusion.6), channel_id=1, source_target_pairs={{0,8},{4,12},{8,0},{12,4},{16,24},{20,28},{24,16},{28,20},{1,9},{5... | collective-permute-start | bytes 663560 | tf_op jit(solution)/shard_map/ppermute | solution.py:316
  200.1 33.1 %collective-permute-start.21 = (bf16[4,240,384]{2,1,0:T(8,128)(2,1)S(1)}, bf16[4,240,384]{2,1,0:T(8,128)(2,1)S(1)}, u32[]{:S(2)}, u32[]{:S(2)}) collective-permute-start(bf16[4,240,384]{2,1,0:T(8,128)(2,1)S(1)} %pad_maximum_fusion.1), channel_id=1, source_target_pairs={{0,4},{4,0},{8,12},{12,8},{16,20},{20,16},{24,28},{28,24},{1,5},{5... | collective-permute-start | bytes 2211848 | tf_op jit(solution)/shard_map/ppermute | solution.py:316
  200.7 30.3 %collective-permute-start.28 = (bf16[4,192,384]{2,1,0:T(8,128)(2,1)S(1)}, bf16[4,192,384]{2,1,0:T(8,128)(2,1)S(1)}, u32[]{:S(2)}, u32[]{:S(2)}) collective-permute-start(bf16[4,192,384]{2,1,0:T(8,128)(2,1)S(1)} %pad_maximum_fusion.2), channel_id=1, source_target_pairs={{0,4},{4,0},{8,12},{12,8},{16,20},{20,16},{24,28},{28,24},{1,5},{5... | collective-permute-start | bytes 1769480 | tf_op jit(solution)/shard_map/ppermute | solution.py:316
  203.8 31.9 %collective-permute-start.12 = (bf16[4,144,384]{2,1,0:T(8,128)(2,1)S(1)}, bf16[4,144,384]{2,1,0:T(8,128)(2,1)S(1)}, u32[]{:S(2)}, u32[]{:S(2)}) collective-permute-start(bf16[4,144,384]{2,1,0:T(8,128)(2,1)S(1)} %pad_maximum_fusion.3), channel_id=1, source_target_pairs={{0,4},{4,0},{8,12},{12,8},{16,20},{20,16},{24,28},{28,24},{1,5},{5... | collective-permute-start | bytes 1327112 | tf_op jit(solution)/shard_map/ppermute | solution.py:316
  (1 other events, 0.9 us)
